TPU v7x, 256 devices: a whole 4x4x8 slice. The times are simulated.
256 devices in a mesh: grp: 8 (over z), seq: 32 (over y, x, core).
Axes of the slice: x: 4, y: 4, z: 8, core: 2. Of those that a mesh axis runs over, the one named last changes fastest.
Arguments:
- queries: bfloat16 [32768, 1232], P(('grp', 'seq')), may hold values from -6 to 6
- key_vectors: bfloat16 [32768, 1232], P(('grp', 'seq')), may hold values from -6 to 6
- value_vectors: bfloat16 [32768, 1232], P(('grp', 'seq')), may hold values from -1 to 3
- output_grad: bfloat16 [32768, 1232], P(('grp', 'seq')), may hold values from -12288 to 12288
- state_in: float32 [11, 112, 112], replicated, may hold values from 38.4 to 64
- norm_in: float32 [11, 112], replicated, may hold values from 38.4 to 64
- grad_state: float32 [11, 112, 112], replicated, may hold values from -1 to 1
- grad_norm: float32 [11, 112], replicated, may hold values from -12 to 12
Outputs:
- query_grad: bfloat16 [32768, 1232], P(('grp', 'seq'))
- key_grad: bfloat16 [32768, 1232], P(('grp', 'seq'))
- value_grad: bfloat16 [32768, 1232], P(('grp', 'seq'))
All inputs are finite; a program needn't handle non-finite values.
Results may differ from a plain program's by a relative error of at most 0.006.
Values sent between devices are 32-bit elements; how exact they have to be, the bound alone decides.
A program may use at most 128 MiB of HBM per device.

v0:
```python
import jax
import jax.numpy as jnp
from jax import lax
from jax.sharding import PartitionSpec as P


def entering(x, axis, combine, identity, reverse):
    length, index = (lax.axis_size(axis), lax.axis_index(axis))
    everything = jax.tree.map(lambda part: lax.all_gather(part, axis), x)
    start = jax.tree.map(
        lambda part, zero: jnp.broadcast_to(jnp.asarray(zero, part.dtype), part.shape), x, identity
    )

    def step(k, before):
        at = length - 1 - k if reverse else k
        reached = at > index if reverse else at < index
        new = combine(before, jax.tree.map(lambda part: part[at], everything))
        return jax.tree.map(lambda a, b: jnp.where(reached, a, b), new, before)

    return lax.fori_loop(0, length, step, start)


def combine_sums(earlier, later):
    return jax.tree.map(jnp.add, earlier, later)


def select_groups(stacked, weights):
    state_all, norm_all = stacked
    return (
        jnp.einsum("g,ghde->hde", weights, state_all, precision=lax.Precision.HIGHEST),
        jnp.einsum("g,ghd->hd", weights, norm_all, precision=lax.Precision.HIGHEST),
    )


def per_device(
    queries, key_vectors, value_vectors, output_grad, state_in, norm_in, grad_state, grad_norm
):
    highest = lax.Precision.HIGHEST
    length = queries.shape[0]
    heads = state_in.shape[0]
    width = state_in.shape[1]
    groups = lax.axis_size("grp")
    group_index = lax.axis_index("grp")
    group_ids = lax.iota(jnp.int32, groups)
    query_feat = jnp.maximum(queries, 0).reshape(length, heads, width)
    key_feat = jnp.maximum(key_vectors, 0).reshape(length, heads, width)
    value_heads = value_vectors.reshape(length, heads, width)
    query_wide = query_feat.astype(jnp.float32)
    key_wide = key_feat.astype(jnp.float32)
    value_wide = value_heads.astype(jnp.float32)
    block_state = jnp.einsum(
        "thd,the->hde", key_feat, value_heads, preferred_element_type=jnp.float32
    )
    block_norm = jnp.sum(key_wide, axis=0)
    empty = (jnp.zeros_like(block_state), jnp.zeros_like(block_norm))
    inner = entering((block_state, block_norm), "seq", combine_sums, empty, False)
    group_total = lax.psum((block_state, block_norm), "seq")
    every_group = (
        lax.all_gather(group_total[0][None], "grp", axis=0, tiled=True),
        lax.all_gather(group_total[1][None], "grp", axis=0, tiled=True),
    )
    outer = select_groups(every_group, (group_ids < group_index).astype(jnp.float32))
    prefix_state = state_in + outer[0] + inner[0]
    prefix_norm = norm_in + outer[1] + inner[1]
    positions = lax.iota(jnp.int32, length)
    causal = (positions[:, None] >= positions[None, :])[None]
    scores = jnp.einsum("thd,shd->hts", query_feat, key_feat, preferred_element_type=jnp.float32)
    masked = jnp.where(causal, scores, 0.0)
    denominator = (
        1.0
        + jnp.einsum("thd,hd->ht", query_wide, prefix_norm, precision=highest)
        + jnp.sum(masked, axis=2)
    )
    scores_low = masked.astype(jnp.bfloat16)
    numerator = jnp.einsum(
        "thd,hde->hte", query_wide, prefix_state, precision=highest
    ) + jnp.einsum("hts,she->hte", scores_low, value_heads, preferred_element_type=jnp.float32)
    output = numerator / denominator[:, :, None]
    grad_wide = output_grad.reshape(length, heads, width).astype(jnp.float32).transpose(1, 0, 2)
    num_grad = grad_wide / denominator[:, :, None]
    den_grad = -jnp.sum(grad_wide * output, axis=2) / denominator
    num_grad_low = num_grad.astype(jnp.bfloat16)
    carry_state = jnp.einsum(
        "thd,hte->hde", query_feat, num_grad_low, preferred_element_type=jnp.float32
    )
    carry_sum = jnp.einsum("thd,ht->hd", query_wide, den_grad, precision=highest)
    inner_back = entering((carry_state, carry_sum), "seq", combine_sums, empty, True)
    group_back = lax.psum((carry_state, carry_sum), "seq")
    every_back = (
        lax.all_gather(group_back[0][None], "grp", axis=0, tiled=True),
        lax.all_gather(group_back[1][None], "grp", axis=0, tiled=True),
    )
    outer_back = select_groups(every_back, (group_ids > group_index).astype(jnp.float32))
    suffix_state = grad_state + outer_back[0] + inner_back[0]
    suffix_norm = grad_norm + outer_back[1] + inner_back[1]
    mixed = (
        jnp.einsum("hte,she->hts", num_grad_low, value_heads, preferred_element_type=jnp.float32)
        + den_grad[:, :, None]
    )
    mixed_low = jnp.where(causal, mixed, 0.0).astype(jnp.bfloat16)
    query_part = (
        jnp.einsum("hte,hde->htd", num_grad, prefix_state, precision=highest)
        + den_grad[:, :, None] * prefix_norm[:, None, :]
        + jnp.einsum("hts,shd->htd", mixed_low, key_feat, preferred_element_type=jnp.float32)
    )
    key_part = (
        jnp.einsum("she,hde->hsd", value_wide, suffix_state, precision=highest)
        + suffix_norm[:, None, :]
        + jnp.einsum("hts,thd->hsd", mixed_low, query_feat, preferred_element_type=jnp.float32)
    )
    value_part = jnp.einsum("shd,hde->hse", key_wide, suffix_state, precision=highest) + jnp.einsum(
        "hts,hte->hse", scores_low, num_grad_low, preferred_element_type=jnp.float32
    )

    def to_tokens(part):
        return part.transpose(1, 0, 2).reshape(length, heads * width)

    query_grad = jnp.where(queries > 0, to_tokens(query_part), 0.0).astype(jnp.bfloat16)
    key_grad = jnp.where(key_vectors > 0, to_tokens(key_part), 0.0).astype(jnp.bfloat16)
    value_grad = to_tokens(value_part).astype(jnp.bfloat16)
    return (query_grad, key_grad, value_grad)


def solution(mesh):
    in_specs = (
        P(("grp", "seq"), None),
        P(("grp", "seq"), None),
        P(("grp", "seq"), None),
        P(("grp", "seq"), None),
        P(),
        P(),
        P(),
        P(),
    )
    out_specs = (P(("grp", "seq"), None), P(("grp", "seq"), None), P(("grp", "seq"), None))
    return jax.shard_map(
        per_device, mesh=mesh, in_specs=in_specs, out_specs=out_specs, check_vma=False
    )
```

profile of v0, /device:TPU:1, one launch (start us, length us, event | category | flops | bytes accessed | tf_op | source)
XLA Modules:
  0.0 621.2 jit_solution(16000607201926535860)
XLA Ops:
  10.8 67.3 %psum.28 = f32[1,11,112]{2,1,0:T(8,128)S(1)} all-reduce(f32[1,11,112]{2,1,0:T(8,128)S(1)} %broadcast_in_dim.50), channel_id=1, replica_groups=mesh['grp'=8,'seq'=32] {'seq'}, use_global_device_ids=true, to_apply=%region_1.2 | all-reduce | flops 1232 | bytes 9856 | tf_op jit(solution)/shard_map/psum | solution.py:57
  78.1 22.8 %all_gather.36 = f32[8,11,112]{2,1,0:T(8,128)S(1)} all-gather(f32[1,11,112]{2,1,0:T(8,128)S(1)} %psum.28), channel_id=1, replica_groups=mesh['grp'=8,'seq'=32] {'grp'}, dimensions={0}, use_global_device_ids=true | all-gather | bytes 44352 | tf_op jit(solution)/shard_map/all_gather | solution.py:60
  100.9 30.9 %all_gather.40 = f32[32,11,112]{2,1,0:T(8,128)S(1)} all-gather(f32[1,11,112]{2,1,0:T(8,128)S(1)} %broadcast_in_dim.50), channel_id=1, replica_groups=mesh['grp'=8,'seq'=32] {'seq'}, dimensions={0}, use_global_device_ids=true | all-gather | bytes 162624 | tf_op jit(solution)/shard_map/all_gather | solution.py:9
  133.4 41.9 %while.34 = (s32[]{:T(128)}, f32[11,112,112]{2,1,0:T(8,128)S(1)}, f32[11,112]{1,0:T(8,128)S(1)}, s32[]{:T(128)}, f32[32,11,112,112]{3,2,1,0:T(8,128)}, /*index=5*/f32[32,11,112]{2,1,0:T(8,128)S(1)}, s32[]{:T(128)}, s32[]{:T(128)}) while((s32[]{:T(128)}, f32[11,112,112]{2,1,0:T(8,128)S(1)}, f32[11,112]{1,0:T(8,128)S(1)}, s32[]{:T(128)}, ...), condition=%wide.region_3.4_spmd.clone, body=%wide.region_2.3_spmd.clone.sunk | while | flops 417652 | bytes 1670707 | solution.py:20
  133.4 1.3 add_select_fusion.8
  176.9 83.3 %all-gather.15.cloned.1.call-done = f32[352,112,112]{2,1,0:T(8,128)} async-done(((f32[11,112,112]{2,1,0:T(8,128)}), f32[352,112,112]{2,1,0:T(8,128)}) %all-gather.15.cloned.1.call-update) | async-done | bytes 17661968 | tf_op jit(solution)/shard_map/all_gather | solution.py:9
  260.9 118.0 %all-reduce.3.cloned.1.call-done = (f32[1,11,112,112]{3,2,1,0:T(8,128)}, f32[1,11,112,112]{3,2,1,0:T(8,128)}) async-done(((f32[1,11,112,112]{3,2,1,0:T(8,128)}, f32[1,11,112,112]{3,2,1,0:T(8,128)}), (f32[1,11,112,112]{3,2,1,0:T(8,128)}, f32[1,11,112,112]{3,2,1,0:T(8,128)})) %all-reduce.3.cloned.1.call-update) | async-done | bytes 1103888 | tf_op jit(solution)/shard_map/psum | solution.py:57
  379.3 2.2 fusion.20
  381.5 61.5 %all-gather.9.cloned.1.call-done = f32[8,11,112,112]{3,2,1,0:T(8,128)} async-done(((f32[1,11,112,112]{3,2,1,0:T(8,128)}), f32[8,11,112,112]{3,2,1,0:T(8,128)}) %all-gather.9.cloned.1.call-update) | async-done | bytes 4415504 | tf_op jit(solution)/shard_map/all_gather | solution.py:59
  443.0 6.1 fusion.2
  450.0 1.9 fusion.13
  452.5 25.3 %all-gather.3 = f32[32,11,112]{2,1,0:T(8,128)S(1)} all-gather(f32[1,11,112]{2,1,0:T(8,128)S(1)} %bitcast.142), channel_id=4, replica_groups=mesh['grp'=8,'seq'=32] {'seq'}, dimensions={0}, use_global_device_ids=true | all-gather | bytes 162624 | tf_op jit(solution)/shard_map/all_gather | solution.py:9
  477.8 42.3 %while.35 = (s32[]{:T(128)}, f32[11,112,112]{2,1,0:T(8,128)S(1)}, f32[11,112]{1,0:T(8,128)S(1)}, s32[]{:T(128)}, f32[32,11,112,112]{3,2,1,0:T(8,128)}, /*index=5...) while((s32[]{:T(128)}, f32[11,112,112]{2,1,0:T(8,128)S(1)}, ...), condition=%wide.region_9.10_spmd.clone, body=%wide.region_8.9_spmd.clone.sunk | while | flops 417656 | bytes 1670769 | solution.py:20
  477.8 1.3 add_select_fusion.10
  479.2 1.3 add_select_fusion.10
  484.5 1.3 add_select_fusion.10
  485.8 1.3 add_select_fusion.10
  492.4 1.3 add_select_fusion.10
  496.4 1.3 add_select_fusion.10
  497.7 1.3 add_select_fusion.10
  520.1 63.1 %psum.31 = f32[1,11,112]{2,1,0:T(8,128)S(1)} all-reduce(f32[1,11,112]{2,1,0:T(8,128)S(1)} %bitcast.143), channel_id=1, replica_groups=mesh['grp'=8,'seq'=32] {'seq'}, use_global_device_ids=true, to_apply=%region_10.11 | all-reduce | flops 1232 | bytes 9856 | tf_op jit(solution)/shard_map/psum | solution.py:88
  583.3 18.7 %all_gather.47 = f32[8,11,112]{2,1,0:T(8,128)S(1)} all-gather(f32[1,11,112]{2,1,0:T(8,128)S(1)} %psum.31), channel_id=1, replica_groups=mesh['grp'=8,'seq'=32] {'grp'}, dimensions={0}, use_global_device_ids=true | all-gather | bytes 44352 | tf_op jit(solution)/shard_map/all_gather | solution.py:91
  603.6 6.1 fusion
  609.8 1.5 fusion.12
  (191 shorter events, 85.9 us)
Async XLA Ops:
  7.2 1.1 copy-start
  7.2 126.2 %all-gather.13.cloned.1.call-start = ((), (), s32[]{:S(2)}) async-start(), calls=%async_computation.2 | async-start | bytes 20815872 | tf_op jit(solution)/shard_map/all_gather | solution.py:9
  9.5 250.7 %all-gather.15.cloned.1.call-start = ((), (), s32[]{:S(2)}) async-start(), calls=%async_computation.3 | async-start | bytes 20815872 | tf_op jit(solution)/shard_map/all_gather | solution.py:9
  133.3 42.0 %copy-start.9 = (f32[11,112]{1,0:T(8,128)S(1)}, f32[11,112]{1,0:T(8,128)}, u32[]{:S(2)}) copy-start(f32[11,112]{1,0:T(8,128)} %param.17) | copy-start | bytes 14788
  133.4 42.3 %copy-start.12 = (bf16[128,1232]{0,1:T(8,128)(2,1)S(1)}, bf16[128,1232]{0,1:T(8,128)(2,1)}, u32[]{:S(2)}) copy-start(bf16[128,1232]{0,1:T(8,128)(2,1)} %param.15) | copy-start | bytes 946180
  260.2 118.8 %all-reduce.3.cloned.1.call-start = ((), (), s32[]{:S(2)}) async-start(), calls=%async_computation.4 | async-start | bytes 2523136 | tf_op jit(solution)/shard_map/psum | solution.py:57
  260.9 182.1 %all-gather.9.cloned.1.call-start = ((), (), s32[]{:S(2)}) async-start(), calls=%async_computation | async-start | bytes 5677056 | tf_op jit(solution)/shard_map/all_gather | solution.py:59
  378.9 224.6 %all-gather.11.cloned.1.call-start = ((), (), s32[]{:S(2)}) async-start(), calls=%async_computation.1 | async-start | bytes 5677056 | tf_op jit(solution)/shard_map/all_gather | solution.py:90
  449.1 0.9 copy-start.7
  477.8 124.3 %copy-start.10 = (f32[11,112]{1,0:T(8,128)S(1)}, f32[11,112]{1,0:T(8,128)}, u32[]{:S(2)}) copy-start(f32[11,112]{1,0:T(8,128)} %param.19) | copy-start | bytes 14788
  477.8 124.3 %copy-start.13 = (bf16[128,1232]{0,1:T(8,128)(2,1)S(1)}, bf16[128,1232]{0,1:T(8,128)(2,1)}, u32[]{:S(2)}) copy-start(bf16[128,1232]{0,1:T(8,128)(2,1)} %param.15) | copy-start | bytes 946180
  602.1 7.6 %copy-start.2 = (f32[11,112,112]{2,1,0:T(8,128)S(1)}, f32[11,112,112]{2,1,0:T(8,128)}, u32[]{:S(2)}) copy-start(f32[11,112,112]{2,1,0:T(8,128)} %param.18) | copy-start | bytes 1655812
  602.5 0.7 copy-start.3
  603.5 8.3 %copy-start.1 = (bf16[128,1232]{0,1:T(8,128)(2,1)S(1)}, bf16[128,1232]{0,1:T(8,128)(2,1)}, u32[]{:S(2)}) copy-start(bf16[128,1232]{0,1:T(8,128)(2,1)} %param.13) | copy-start | bytes 946180
  603.6 6.2 copy-start.6
  609.7 2.9 copy-start.8
  609.8 2.9 copy-start.11
  609.8 2.9 copy-start.14
  609.8 3.7 copy-start.4
  611.3 2.6 copy-start.5
Sparse Core Ops, SparseCore 0:
  10.6 90.2 all-gather.12
  177.0 83.1 all-gather.14
  264.4 114.4 all-reduce.2
  380.6 62.3 all-gather.8
  444.6 61.3 all-gather.10
where the time goes:
time: 631 us; the launch traced here: 621 us
  waiting for transfers between devices  264 us (42%)
  blocking collectives  228 us (36%)
  other arithmetic  86.8 us (14%)
  matrix products  24.3 us (4%)
  between operations  14.1 us (2%)
    psum x1, waiting for transfers between devices, per_device(): group_total = lax.psum((block_state, block_norm), 'seq')  118 us
    all_gather x2, waiting for transfers between devices, entering(): everything = jax.tree.map(lambda part: lax.all_gather(part, axis), x)  83.3 us
    select_n x128, other arithmetic, step(): return jax.tree.map(lambda a, b: jnp.where(reached, a, b), new, before)  81.9 us
    psum x1, blocking collectives, per_device(): group_total = lax.psum((block_state, block_norm), 'seq')  67.3 us
    psum x1, blocking collectives, per_device(): group_back = lax.psum((carry_state, carry_sum), 'seq')  63.1 us
    all_gather x1, waiting for transfers between devices, per_device(): lax.all_gather(group_total[0][None], 'grp', axis=0, tiled=True)  61.5 us
    all_gather x2, blocking collectives, entering(): everything = jax.tree.map(lambda part: lax.all_gather(part, axis), x)  56.2 us
    all_gather x1, blocking collectives, per_device(): lax.all_gather(group_total[1][None], 'grp', axis=0, tiled=True)  22.8 us
  transfers between devices with their start and end apart: 5, of which 3 were waited for; matrix products, arithmetic and copies ran while one was open for 9% of the time, Pallas kernels for 0%

commit v1 on v0

v1 whole, which is shorter than its diff:
```python
import functools
import math

import jax
import jax.numpy as jnp
from jax import lax
from jax.experimental import pallas as pl
from jax.experimental.pallas import tpu as pltpu
from jax.sharding import PartitionSpec as P

MESH = pl.DeviceIdType.MESH
F32 = jnp.float32
BF16 = jnp.bfloat16
NN = (((1,), (0,)), ((), ()))
NT = (((1,), (1,)), ((), ()))
TN = (((0,), (0,)), ((), ()))
LANES = 128


def mm(x, y, dims):
    return lax.dot_general(x, y, dims, preferred_element_type=F32)


def split(x):
    high = x.astype(BF16)
    return high, (x - high.astype(F32)).astype(BF16)


class Place:
    def __init__(self, groups, chips):
        self.groups, self.chips = groups, chips
        self.side = math.isqrt(chips)
        self.z = lax.axis_index("grp")
        seq = lax.axis_index("seq")
        self.p, self.c = seq // 2, seq % 2
        self.y, self.x = self.p // self.side, self.p % self.side
        side = self.side
        offsets = [(dy, dx) for dy in range(side) for dx in range(side) if dy or dx]
        self.plane = sorted(offsets, key=lambda o: min(o[0], side - o[0]) + min(o[1], side - o[1]))
        self.column = sorted(range(1, groups), key=lambda d: min(d, groups - d))

    def chip(self, offset, sign):
        side = self.side
        y = (self.y + sign * offset[0] + side) % side
        x = (self.x + sign * offset[1] + side) % side
        return y * side + x

    def plane_to(self, k):
        return self.chip(self.plane[k], 1)

    def plane_from(self, k):
        return self.chip(self.plane[k], -1)

    def z_to(self, k):
        return (self.z + self.column[k]) % self.groups

    def z_from(self, k):
        return (self.z + self.groups - self.column[k]) % self.groups

    def chip_id(self, p):
        return (self.z, p * 2 + self.c)

    def z_id(self, z):
        return (z, self.p * 2 + self.c)

    def core_id(self):
        return (self.z, self.p * 2 + 1 - self.c)


def remote(src, dst, send, recv, device):
    return pltpu.make_async_remote_copy(
        src_ref=src, dst_ref=dst, send_sem=send, recv_sem=recv, device_id=device, device_id_type=MESH
    )


def flag(condition):
    return condition.astype(jnp.int32).astype(F32)


class SmallScan:
    def __init__(self, at, later, refs):
        self.at, self.later = at, later
        self.own, self.other, self.chip, self.plane, self.column, self.total = refs[:6]
        self.core_s, self.plane_s, self.column_s = refs[6:]
        self.sent = []

    def start(self, copy):
        copy.start()
        self.sent.append(copy)

    def core_copy(self):
        sems = self.core_s
        return remote(self.own, self.other, sems.at[0, 0], sems.at[1, 0], self.at.core_id())

    def core_send(self):
        self.start(self.core_copy())

    def plane_copy(self, k, slot, device):
        sems = self.plane_s
        return remote(self.chip, self.plane.at[slot], sems.at[0, k], sems.at[1, k], device)

    def plane_send(self):
        at = self.at
        self.core_copy().wait_recv()
        both = self.own[...] + self.other[...]
        self.chip[...] = both
        for k in reversed(range(len(at.plane))):
            self.start(self.plane_copy(k, at.p, at.chip_id(at.plane_to(k))))
        self.plane[at.p] = both

    def column_copy(self, k, slot, device):
        sems = self.column_s
        return remote(
            self.column.at[self.at.z], self.column.at[slot], sems.at[0, k], sems.at[1, k], device
        )

    def column_send(self):
        at = self.at
        for k in range(len(at.plane)):
            source = at.plane_from(k)
            self.plane_copy(k, source, at.chip_id(source)).wait_recv()
        everything = self.plane[0]
        for p in range(1, at.chips):
            everything = everything + self.plane[p]
        self.column[at.z] = everything
        for k in reversed(range(len(at.column))):
            self.start(self.column_copy(k, at.z, at.z_id(at.z_to(k))))
        reached = (lambda i, me: i > me) if self.later else (lambda i, me: i < me)
        near = flag(at.c == (0 if self.later else 1)) * self.other[...]
        for p in range(at.chips):
            near = near + flag(reached(p, at.p)) * self.plane[p]
        self.total[...] = self.total[...] + near

    def finish(self):
        at = self.at
        for k in range(len(at.column)):
            source = at.z_from(k)
            self.column_copy(k, source, at.z_id(source)).wait_recv()
        reached = (lambda i, me: i > me) if self.later else (lambda i, me: i < me)
        far = flag(reached(0, at.z)) * self.column[0]
        for z in range(1, at.groups):
            far = far + flag(reached(z, at.z)) * self.column[z]
        self.total[...] = self.total[...] + far

    def drain(self):
        for copy in self.sent:
            copy.wait_send()


class LargeScan:
    def __init__(self, at, later, share, refs):
        self.at, self.later, self.share = at, later, share
        self.own, self.other, self.chip, self.plane, self.column, self.back, self.result = refs[:7]
        self.core_s, self.plane_s, self.column_s, self.back_s, self.pass_s = refs[7:]
        self.half = share * at.chips
        self.sent = []

    def start(self, copy):
        copy.start()
        self.sent.append(copy)

    def piece(self, p):
        return pl.ds((self.at.c * self.at.chips + p) * self.share, self.share)

    def core_copy(self, k, core):
        part = pl.ds(core * self.half, self.half)
        sems = self.core_s
        return remote(
            self.own.at[part], self.other.at[part], sems.at[0, k], sems.at[1, k], self.at.core_id()
        )

    def core_send(self):
        self.start(self.core_copy(0, 1 - self.at.c))
        self.start(self.core_copy(1, self.at.c))

    def plane_copy(self, k, src, slot, device):
        sems = self.plane_s
        return remote(self.chip.at[src], self.plane.at[slot], sems.at[0, k], sems.at[1, k], device)

    def plane_send(self):
        at = self.at
        self.core_copy(0, at.c).wait_recv()
        for k in reversed(range(len(at.plane))):
            target = at.plane_to(k)
            part = self.piece(target)
            self.chip[target] = self.own[part] + self.other[part]
            self.start(self.plane_copy(k, target, at.p, at.chip_id(target)))
        part = self.piece(at.p)
        self.plane[at.p] = self.own[part] + self.other[part]

    def column_copy(self, k, slot, device):
        sems = self.column_s
        return remote(
            self.column.at[self.at.z], self.column.at[slot], sems.at[0, k], sems.at[1, k], device
        )

    def column_send(self):
        at = self.at
        for k in range(len(at.plane)):
            source = at.plane_from(k)
            self.plane_copy(k, source, source, at.chip_id(source)).wait_recv()
        order = list(range(at.chips))
        if self.later:
            order.reverse()
        running = jnp.zeros(self.column.shape[1:], F32)
        for p in order:
            self.back[p] = running
            running = running + self.plane[p]
        self.column[at.z] = running
        for k in reversed(range(len(at.column))):
            self.start(self.column_copy(k, at.z, at.z_id(at.z_to(k))))

    def back_copy(self, k, src, owner, device):
        sems = self.back_s
        return remote(
            self.back.at[src], self.result.at[self.piece(owner)], sems.at[0, k], sems.at[1, k], device
        )

    def pass_copy(self, k, core, owner):
        part = pl.ds((core * self.at.chips + owner) * self.share, self.share)
        sems = self.pass_s
        return remote(
            self.result.at[part], self.result.at[part], sems.at[0, k], sems.at[1, k], self.at.core_id()
        )

    def back_send(self):
        at = self.at
        for k in range(len(at.column)):
            source = at.z_from(k)
            self.column_copy(k, source, at.z_id(source)).wait_recv()
        reached = (lambda i, me: i > me) if self.later else (lambda i, me: i < me)
        far = flag(reached(0, at.z)) * self.column[0]
        for z in range(1, at.groups):
            far = far + flag(reached(z, at.z)) * self.column[z]
        for k in reversed(range(len(at.plane))):
            target = at.plane_to(k)
            self.back[target] = self.back[target] + far
            self.start(self.back_copy(k, target, at.p, at.chip_id(target)))
        self.result[self.piece(at.p)] = self.back[at.p] + far
        self.start(self.pass_copy(len(at.plane), at.c, at.p))

    def back_pass(self):
        at = self.at
        for k in range(len(at.plane)):
            source = at.plane_from(k)
            self.back_copy(k, source, source, at.chip_id(source)).wait_recv()
            self.start(self.pass_copy(k, at.c, source))

    def core_rest(self):
        self.core_copy(1, 1 - self.at.c).wait_recv()

    def finish(self):
        at = self.at
        for k in range(len(at.plane)):
            self.pass_copy(k, 1 - at.c, at.plane_from(k)).wait_recv()
        self.pass_copy(len(at.plane), 1 - at.c, at.p).wait_recv()

    def drain(self):
        for copy in self.sent:
            copy.wait_send()


def kernel(groups, chips, heads, width, share, *refs):
    hbm_in, hbm_out, refs = refs[:8], refs[8:11], refs[11:]
    q_v, k_v, v_v, g_v, st_v, nm_v, gs_v, gn_v = refs[:8]
    dq_v, dk_v, dv_v = refs[8:11]
    a_s, b_s, v_s, g_s, ub_s, ul_s, ua_s, pt_s, sh_s, sl_s, rh_s, rl_s = refs[11:23]
    den_s, num_s, c_s, kp_s, vp_s, init_s, init_r = refs[23:30]
    load_s, store_s = refs[30:32]
    small = refs[32:50]
    large = refs[50:]
    at = Place(groups, chips)
    n_scan = SmallScan(at, False, small[:9])
    m_scan = SmallScan(at, True, small[9:])
    b_scan = LargeScan(at, False, share, large[:12])
    c_scan = LargeScan(at, True, share, large[12:])
    tokens = k_v.shape[0]
    rows = width // 8

    barrier = pltpu.get_barrier_semaphore()
    for k in range(len(at.plane)):
        pl.semaphore_signal(
            barrier, inc=1, device_id=at.chip_id(at.plane_to(k)), device_id_type=MESH
        )
    for k in range(len(at.column)):
        pl.semaphore_signal(barrier, inc=1, device_id=at.z_id(at.z_to(k)), device_id_type=MESH)
    pl.semaphore_signal(barrier, inc=1, device_id=at.core_id(), device_id_type=MESH)

    loads = [
        pltpu.make_async_copy(src, dst, load_s.at[i])
        for i, (src, dst) in enumerate(zip(hbm_in, (q_v, k_v, v_v, g_v, st_v, nm_v, gs_v, gn_v)))
    ]
    for i in (1, 2, 0, 3, 5, 4, 7, 6):
        loads[i].start()

    lane = lax.broadcasted_iota(jnp.int32, (tokens, LANES), 1)
    row = lax.broadcasted_iota(jnp.int32, (tokens, LANES), 0)
    lower = row >= lane
    upper = row <= lane
    ones_pair = jnp.where((lane == width) | (lane == width + 1), 1.0, 0.0).astype(BF16)
    blank = jnp.zeros((tokens, LANES), BF16)
    for h in range(heads):
        a_s[h] = blank
        b_s[h] = blank
        v_s[h] = ones_pair
        g_s[h] = blank
        for ref in (sh_s, sl_s, rh_s, rl_s):
            ref[h, width:, :] = jnp.zeros((LANES - width, LANES), BF16)
    spare = b_scan.own.shape[0] - heads * rows
    for scan in (b_scan, c_scan):
        scan.own[heads * rows :] = jnp.zeros((spare, 8, LANES), F32)
    for scan in (n_scan, m_scan):
        scan.own[...] = jnp.zeros(scan.own.shape, F32)
        scan.total[...] = jnp.zeros(scan.own.shape, F32)

    def tiles(h):
        return slice(h * rows, (h + 1) * rows)

    def columns(h):
        return slice(h * width, (h + 1) * width)

    loads[1].wait()
    for h in range(heads):
        b_s[h, :, :width] = jnp.maximum(k_v[:, columns(h)], 0)
    some = jnp.ones((8, tokens), BF16)
    for h in range(heads):
        n_scan.own[h : h + 1, :] = mm(some, b_s[h], NN)[0:1]
    pl.semaphore_wait(barrier, len(at.plane) + len(at.column) + 1)
    n_scan.core_send()

    loads[2].wait()
    for h in range(heads):
        v_s[h, :, :width] = v_v[:, columns(h)]
    for h in range(heads):
        b_scan.own[tiles(h)] = mm(b_s[h], v_s[h], TN)[:width].reshape(rows, 8, LANES)
    b_scan.core_send()
    n_scan.plane_send()

    loads[0].wait()
    for h in range(heads):
        a_s[h, :, :width] = jnp.maximum(q_v[:, columns(h)], 0)
    b_scan.plane_send()

    loads[5].wait()
    n_scan.total[:heads, :width] = nm_v[...]
    loads[7].wait()
    m_scan.total[:heads, :width] = gn_v[...]

    loads[3].wait()
    for h in range(heads):
        g_s[h, :, :width] = g_v[:, columns(h)]
    for h in range(heads):
        scores = jnp.where(lower, mm(a_s[h], b_s[h], NT), 0.0)
        den_s[h] = jnp.broadcast_to(1.0 + jnp.sum(scores, axis=1, keepdims=True), (tokens, LANES))
        num_s[h] = mm(scores.astype(BF16), v_s[h], NN)
        pt_s[h] = jnp.where(upper, mm(b_s[h], a_s[h], NT), 0.0).astype(BF16)
    n_scan.column_send()

    loads[4].wait()
    loads[6].wait()
    for init, state in ((init_s, st_v), (init_r, gs_v)):
        init[...] = jnp.zeros(init.shape, F32)
        for h in range(heads):
            init[tiles(h), :, :width] = state[h].reshape(rows, 8, width)
    b_scan.core_rest()
    init_s[...] = init_s[...] + flag(at.c == 1) * b_scan.other[: heads * rows]

    b_scan.column_send()

    n_scan.finish()
    for h in range(heads):
        high, low = split(n_scan.total[h : h + 1, :])
        both = mm(a_s[h], jnp.broadcast_to(high, (LANES, LANES)), NT) + mm(
            a_s[h], jnp.broadcast_to(low, (LANES, LANES)), NT
        )
        inverse = 1.0 / (den_s[h] + both)
        den_s[h] = inverse
        ub_s[h], ul_s[h] = split(g_s[h].astype(F32) * inverse)
    for h in range(heads):
        c_scan.own[tiles(h)] = mm(a_s[h], ub_s[h], TN)[:width].reshape(rows, 8, LANES)
    c_scan.core_send()
    for h in range(heads):
        vp_s[h] = mm(pt_s[h], ub_s[h], NN)
    c_scan.plane_send()
    b_scan.back_send()
    c_scan.core_rest()
    init_r[...] = init_r[...] + flag(at.c == 0) * c_scan.other[: heads * rows]
    b_scan.back_pass()
    c_scan.column_send()
    b_scan.finish()

    for h in range(heads):
        state = (b_scan.result[tiles(h)] + init_s[tiles(h)]).reshape(width, LANES)
        sh_s[h, :width, :], sl_s[h, :width, :] = split(state)
    for h in range(heads):
        numerator = mm(a_s[h], sh_s[h], NN) + mm(a_s[h], sl_s[h], NN) + num_s[h]
        inverse = den_s[h]
        scaled = g_s[h].astype(F32) * inverse
        c = -jnp.sum(scaled * (numerator * inverse), axis=1, keepdims=True)
        c_s[h] = jnp.broadcast_to(c, (tokens, LANES))
        m_scan.own[h : h + 1, :] = jnp.sum(c * a_s[h].astype(F32), axis=0, keepdims=True)
    m_scan.core_send()
    m_scan.plane_send()

    for h in range(heads):
        high, low = split(c_s[h])
        ua_s[h] = jnp.where(lane == width, high, jnp.where(lane == width + 1, low, ub_s[h]))
    for h in range(heads):
        mixed = jnp.where(lower, mm(ua_s[h], v_s[h], NT), 0.0).astype(BF16)
        part = mm(ub_s[h], sh_s[h], NT) + mm(ub_s[h], sl_s[h], NT) + mm(ul_s[h], sh_s[h], NT)
        part = part + c_s[h] * n_scan.total[h : h + 1, :] + mm(mixed, b_s[h], NN)
        part = jnp.where(a_s[h] > 0, part, 0.0)
        dq_v[:, columns(h)] = part[:, :width].astype(BF16)
        turned = jnp.where(upper, mm(v_s[h], ua_s[h], NT), 0.0).astype(BF16)
        kp_s[h] = mm(turned, a_s[h], NN)
    stores = [
        pltpu.make_async_copy(src, dst, store_s.at[i])
        for i, (src, dst) in enumerate(zip((dq_v, dk_v, dv_v), hbm_out))
    ]
    stores[0].start()
    c_scan.back_send()
    m_scan.column_send()
    c_scan.back_pass()
    c_scan.finish()

    for h in range(heads):
        state = (c_scan.result[tiles(h)] + init_r[tiles(h)]).reshape(width, LANES)
        rh_s[h, :width, :], rl_s[h, :width, :] = split(state)
    for h in range(heads):
        part = vp_s[h] + mm(b_s[h], rh_s[h], NN) + mm(b_s[h], rl_s[h], NN)
        dv_v[:, columns(h)] = part[:, :width].astype(BF16)
    stores[2].start()
    for h in range(heads):
        kp_s[h] = kp_s[h] + mm(v_s[h], rh_s[h], NT) + mm(v_s[h], rl_s[h], NT)
    m_scan.finish()
    for h in range(heads):
        part = jnp.where(b_s[h] > 0, kp_s[h] + m_scan.total[h : h + 1, :], 0.0)
        dk_v[:, columns(h)] = part[:, :width].astype(BF16)
    stores[1].start()
    for scan in (n_scan, b_scan, m_scan, c_scan):
        scan.drain()
    for copy in stores:
        copy.wait()


def small_scratch(groups, chips):
    one = pltpu.VMEM((16, LANES), F32)
    sem = pltpu.SemaphoreType.DMA
    return [
        one,
        one,
        one,
        pltpu.VMEM((chips, 16, LANES), F32),
        pltpu.VMEM((groups, 16, LANES), F32),
        one,
        sem((2, 1)),
        sem((2, chips - 1)),
        sem((2, groups - 1)),
    ]


def large_scratch(groups, chips, share):
    whole = pltpu.VMEM((2 * chips * share, 8, LANES), F32)
    plane = pltpu.VMEM((chips, share, 8, LANES), F32)
    sem = pltpu.SemaphoreType.DMA
    return [
        whole,
        whole,
        plane,
        plane,
        pltpu.VMEM((groups, share, 8, LANES), F32),
        plane,
        whole,
        sem((2, 2)),
        sem((2, chips - 1)),
        sem((2, groups - 1)),
        sem((2, chips - 1)),
        sem((2, chips)),
    ]


def per_device(groups, chips, *args):
    tokens, columns = args[0].shape
    heads, width = args[4].shape[:2]
    share = -(-(heads * width // 8) // (2 * chips))
    token = pltpu.VMEM((tokens, columns), BF16)
    state = pltpu.VMEM((heads, width, width), F32)
    norm = pltpu.VMEM((heads, width), F32)
    low = pltpu.VMEM((heads, tokens, LANES), BF16)
    square = pltpu.VMEM((heads, LANES, LANES), BF16)
    wide = pltpu.VMEM((heads, tokens, LANES), F32)
    init = pltpu.VMEM((heads * width // 8, 8, LANES), F32)
    sem = pltpu.SemaphoreType.DMA
    scratch = [token] * 4 + [state, norm, state, norm] + [token] * 3
    scratch += [low] * 7 + [square] + [square] * 4
    scratch += [wide] * 5 + [init] * 2 + [sem((8,)), sem((3,))]
    scratch += small_scratch(groups, chips) * 2 + large_scratch(groups, chips, share) * 2
    return pl.pallas_call(
        functools.partial(kernel, groups, chips, heads, width, share),
        out_shape=[jax.ShapeDtypeStruct((tokens, columns), BF16)] * 3,
        in_specs=[pl.BlockSpec(memory_space=pl.ANY)] * 8,
        out_specs=[pl.BlockSpec(memory_space=pl.ANY)] * 3,
        scratch_shapes=scratch,
        compiler_params=pltpu.CompilerParams(
            collective_id=0, has_side_effects=True, vmem_limit_bytes=40 * 2**20
        ),
        name="scan_kernel",
    )(*args)


def solution(mesh):
    groups, chips = mesh.shape["grp"], mesh.shape["seq"] // 2
    tokens = P(("grp", "seq"), None)
    return jax.shard_map(
        functools.partial(per_device, groups, chips),
        mesh=mesh,
        in_specs=(tokens,) * 4 + (P(),) * 4,
        out_specs=(tokens,) * 3,
        check_vma=False,
    )
```

time: 631 us -> 59 us (0.09); the launches traced: 621 us -> 58.8 us
  waiting for transfers between devices: 264 us -> 0 us
  blocking collectives: 228 us -> 0 us
  other arithmetic: 86.8 us -> 0 us
  Pallas kernels: 0 us -> 50.6 us
  matrix products: 24.3 us -> 0 us
  between operations: 14.1 us -> 0.7 us
    all_gather x4 -> x0, waiting for transfers between devices: 145 us -> none  [the longest x2 83.3 us: entering(): everything = jax.tree.map(lambda part: lax.all_gather(part, axis), x)]
    psum x2 -> x0, blocking collectives: 130 us -> none  [the longest x1 67.3 us: per_device(): group_total = lax.psum((block_state, block_norm), 'seq')]
    psum x1 -> x0, waiting for transfers between devices: 118 us -> none  [per_device(): group_total = lax.psum((block_state, block_norm), 'seq')]
    all_gather x4 -> x0, blocking collectives: 97.7 us -> none  [the longest x2 56.2 us: entering(): everything = jax.tree.map(lambda part: lax.all_gather(part, axis), x)]
    select_n x128 -> x0, other arithmetic: 81.9 us -> none  [step(): return jax.tree.map(lambda a, b: jnp.where(reached, a, b), new, before)]
    pallas_call x0 -> x1, Pallas kernels: none -> 50.6 us  [per_device(): pl.pallas_call(functools.partial(kernel, groups, chips, heads, width, sha...]
    dot_general x18 -> x0, matrix products: 24.3 us -> none  [the longest x2 12.2 us: select_groups(): jnp.einsum('g,ghde->hde', weights, state_all, precision=lax.Precision.HIG...]
  transfers between devices with their start and end apart: 5 -> 0, of which waited for: 3 -> 0; matrix products, arithmetic and copies ran while one was open for 9% -> 0% of each run, Pallas kernels for 0% -> 0%
where the time goes in v1:
time: 59 us; the launch traced here: 58.8 us
  Pallas kernels  50.6 us (86%)
  local copies, waits for them, and re-layouts  7.48 us (13%)
  between operations  0.7 us (1%)
    pallas_call x1, Pallas kernels, per_device(): pl.pallas_call(functools.partial(kernel, groups, chips, heads, width, sha...  50.6 us
    unnamed x18, local copies, waits for them, and re-layouts  4.8 us
    pallas_call x3, local copies, waits for them, and re-layouts, per_device(): pl.pallas_call(functools.partial(kernel, groups, chips, heads, width, sha...  2.67 us

profile of v1, /device:TPU:1, one launch (start us, length us, event | category | flops | bytes accessed | tf_op | source)
XLA Modules:
  0.0 58.8 jit_solution(17079285777608602469)
XLA Ops:
  0.6 0.0 copy-start.4
  0.6 1.2 %copy.11.refs_0_ = bf16[128,1232]{1,0:T(8,128)(2,1)S(1)} copy(bf16[128,1232]{0,1:T(8,128)(2,1)} %param.8) | data formatting | bytes 630784 | tf_op args[0]
  1.8 0.0 copy-done.4
  1.8 0.0 copy-start.5
  1.8 0.0 copy-start.6
  1.9 0.2 copy.12.refs_1_
  2.0 0.8 %copy-done.5 = bf16[128,1232]{0,1:T(8,128)(2,1)S(1)} copy-done((bf16[128,1232]{0,1:T(8,128)(2,1)S(1)}, bf16[128,1232]{0,1:T(8,128)(2,1)}, u32[]{:S(2)}) %copy-start.5) | copy-done | bytes 315416
  2.8 0.0 copy-start
  2.8 0.0 copy-start.1
  2.8 0.2 copy.13.refs_2_
  3.0 0.0 copy-done.6
  3.0 0.2 copy.14.refs_3_
  3.2 0.7 %copy-done = f32[11,112,112]{2,1,0:T(8,128)S(1)} copy-done((f32[11,112,112]{2,1,0:T(8,128)S(1)}, f32[11,112,112]{2,1,0:T(8,128)}, u32[]{:S(2)}) %copy-start) | copy-done | bytes 551960
  3.9 0.2 copy-done.1
  4.1 0.0 copy-start.2
  4.1 0.7 %copy-done.2 = f32[11,112]{1,0:T(8,128)S(1)} copy-done((f32[11,112]{1,0:T(8,128)S(1)}, f32[11,112]{1,0:T(8,128)}, u32[]{:S(2)}) %copy-start.2) | copy-done | bytes 4952
  4.8 0.0 copy-start.3
  4.8 0.7 %copy-done.3 = f32[11,112]{1,0:T(8,128)S(1)} copy-done((f32[11,112]{1,0:T(8,128)S(1)}, f32[11,112]{1,0:T(8,128)}, u32[]{:S(2)}) %copy-start.3) | copy-done | bytes 4952
  5.5 50.6 %scan_kernel.1 = (bf16[128,1232]{1,0:T(8,128)(2,1)S(1)}, bf16[128,1232]{1,0:T(8,128)(2,1)S(1)}, bf16[128,1232]{1,0:T(8,128)(2,1)S(1)}) custom-call(bf16[128,1232]{1,0:T(8,128)(2,1)S(1)} %copy.11.refs_0_, bf16[128,1232]{1,0:T(8,128)(2,1)S(1)} %copy.12.refs_1_, bf16[128,1232]{1,0:T(8,128)(2,1)S(1)} %copy.13.refs_2_, bf16[128,1232]{1,0:T(8,128)(2,1)S(1)} %copy.14.refs_3_, ...), custom_call_target="tpu_custom_call" | custom-call | tf_op jit(solution)/shard_map/scan_kernel/pallas_call | solution.py:498
  56.1 0.9 %copy.15 = bf16[128,1232]{0,1:T(8,128)(2,1)} copy(bf16[128,1232]{1,0:T(8,128)(2,1)S(1)} %get-tuple-element.3) | data formatting | bytes 630784 | tf_op jit(solution)/shard_map/scan_kernel/pallas_call | solution.py:498
  57.0 0.9 %copy.16 = bf16[128,1232]{0,1:T(8,128)(2,1)} copy(bf16[128,1232]{1,0:T(8,128)(2,1)S(1)} %get-tuple-element.4) | data formatting | bytes 630784 | tf_op jit(solution)/shard_map/scan_kernel/pallas_call | solution.py:498
  57.9 0.9 %copy.17 = bf16[128,1232]{0,1:T(8,128)(2,1)} copy(bf16[128,1232]{1,0:T(8,128)(2,1)S(1)} %get-tuple-element.5) | data formatting | bytes 630784 | tf_op jit(solution)/shard_map/scan_kernel/pallas_call | solution.py:498
Async XLA Ops:
  0.6 1.2 %copy-start.4 = (bf16[128,1232]{0,1:T(8,128)(2,1)S(1)}, bf16[128,1232]{0,1:T(8,128)(2,1)}, u32[]{:S(2)}) copy-start(bf16[128,1232]{0,1:T(8,128)(2,1)} %param.9) | copy-start | bytes 946180
  1.8 1.0 %copy-start.5 = (bf16[128,1232]{0,1:T(8,128)(2,1)S(1)}, bf16[128,1232]{0,1:T(8,128)(2,1)}, u32[]{:S(2)}) copy-start(bf16[128,1232]{0,1:T(8,128)(2,1)} %param.10) | copy-start | bytes 946180
  1.8 1.1 %copy-start.6 = (bf16[128,1232]{0,1:T(8,128)(2,1)S(1)}, bf16[128,1232]{0,1:T(8,128)(2,1)}, u32[]{:S(2)}) copy-start(bf16[128,1232]{0,1:T(8,128)(2,1)} %param.11) | copy-start | bytes 946180
  2.8 1.1 %copy-start = (f32[11,112,112]{2,1,0:T(8,128)S(1)}, f32[11,112,112]{2,1,0:T(8,128)}, u32[]{:S(2)}) copy-start(f32[11,112,112]{2,1,0:T(8,128)} %refs_4_.1) | copy-start | bytes 1655812
  2.8 1.3 %copy-start.1 = (f32[11,112,112]{2,1,0:T(8,128)S(1)}, f32[11,112,112]{2,1,0:T(8,128)}, u32[]{:S(2)}) copy-start(f32[11,112,112]{2,1,0:T(8,128)} %refs_6_.1) | copy-start | bytes 1655812
  4.1 0.7 %copy-start.2 = (f32[11,112]{1,0:T(8,128)S(1)}, f32[11,112]{1,0:T(8,128)}, u32[]{:S(2)}) copy-start(f32[11,112]{1,0:T(8,128)} %refs_5_.1) | copy-start | bytes 14788
  4.8 0.7 %copy-start.3 = (f32[11,112]{1,0:T(8,128)S(1)}, f32[11,112]{1,0:T(8,128)}, u32[]{:S(2)}) copy-start(f32[11,112]{1,0:T(8,128)} %refs_7_.1) | copy-start | bytes 14788

commit v2 on v1

--- a/solution.py
+++ b/solution.py
@@ -80,8 +80,8 @@
 class SmallScan:
     def __init__(self, at, later, refs):
         self.at, self.later = at, later
-        self.own, self.other, self.chip, self.plane, self.column, self.total = refs[:6]
-        self.core_s, self.plane_s, self.column_s = refs[6:]
+        self.own, self.other, self.chip, self.plane, self.column, self.total, self.flat = refs[:7]
+        self.core_s, self.plane_s, self.column_s = refs[7:]
         self.sent = []
 
     def start(self, copy):
@@ -141,6 +141,8 @@
         for z in range(1, at.groups):
             far = far + flag(reached(z, at.z)) * self.column[z]
         self.total[...] = self.total[...] + far
+        for h in range(self.total.shape[0]):
+            self.flat[h : h + 1, :] = self.total[h]
 
     def drain(self):
         for copy in self.sent:
@@ -261,99 +263,84 @@
 
 
 def kernel(groups, chips, heads, width, share, *refs):
-    hbm_in, hbm_out, refs = refs[:8], refs[8:11], refs[11:]
+    hbm_in, (dq_v, dk_v, dv_v), refs = refs[:8], refs[8:11], refs[11:]
     q_v, k_v, v_v, g_v, st_v, nm_v, gs_v, gn_v = refs[:8]
-    dq_v, dk_v, dv_v = refs[8:11]
-    a_s, b_s, v_s, g_s, ub_s, ul_s, ua_s, pt_s, sh_s, sl_s, rh_s, rl_s = refs[11:23]
-    den_s, num_s, c_s, kp_s, vp_s, init_s, init_r = refs[23:30]
-    load_s, store_s = refs[30:32]
-    small = refs[32:50]
-    large = refs[50:]
+    a_s, b_s, ub_s, ul_s, sh_s, sl_s, pt_s = refs[8:15]
+    num_s, kp_s, vp_s, den_s, c_s, init_s, init_r = refs[15:22]
+    load_s = refs[22]
+    small = refs[23:43]
+    large = refs[43:]
     at = Place(groups, chips)
-    n_scan = SmallScan(at, False, small[:9])
-    m_scan = SmallScan(at, True, small[9:])
+    n_scan = SmallScan(at, False, small[:10])
+    m_scan = SmallScan(at, True, small[10:])
     b_scan = LargeScan(at, False, share, large[:12])
     c_scan = LargeScan(at, True, share, large[12:])
-    tokens = k_v.shape[0]
-    rows = width // 8
-
-    barrier = pltpu.get_barrier_semaphore()
-    for k in range(len(at.plane)):
-        pl.semaphore_signal(
-            barrier, inc=1, device_id=at.chip_id(at.plane_to(k)), device_id_type=MESH
-        )
-    for k in range(len(at.column)):
-        pl.semaphore_signal(barrier, inc=1, device_id=at.z_id(at.z_to(k)), device_id_type=MESH)
-    pl.semaphore_signal(barrier, inc=1, device_id=at.core_id(), device_id_type=MESH)
+    tokens = k_v.shape[1]
+    tall = width // 8
 
     loads = [
         pltpu.make_async_copy(src, dst, load_s.at[i])
         for i, (src, dst) in enumerate(zip(hbm_in, (q_v, k_v, v_v, g_v, st_v, nm_v, gs_v, gn_v)))
     ]
-    for i in (1, 2, 0, 3, 5, 4, 7, 6):
+    loads[1].start()
+    loads[2].start()
+    barrier = pltpu.get_barrier_semaphore()
+    partners = [at.core_id()]
+    partners += [at.chip_id(at.plane_to(k)) for k in range(len(at.plane))]
+    partners += [at.z_id(at.z_to(k)) for k in range(len(at.column))]
+    for partner in partners:
+        pl.semaphore_signal(barrier, inc=1, device_id=partner, device_id_type=MESH)
+    for i in (0, 3, 5, 7, 4, 6):
         loads[i].start()
 
-    lane = lax.broadcasted_iota(jnp.int32, (tokens, LANES), 1)
-    row = lax.broadcasted_iota(jnp.int32, (tokens, LANES), 0)
-    lower = row >= lane
-    upper = row <= lane
-    ones_pair = jnp.where((lane == width) | (lane == width + 1), 1.0, 0.0).astype(BF16)
-    blank = jnp.zeros((tokens, LANES), BF16)
-    for h in range(heads):
-        a_s[h] = blank
-        b_s[h] = blank
-        v_s[h] = ones_pair
-        g_s[h] = blank
-        for ref in (sh_s, sl_s, rh_s, rl_s):
-            ref[h, width:, :] = jnp.zeros((LANES - width, LANES), BF16)
-    spare = b_scan.own.shape[0] - heads * rows
+    upper = lax.broadcasted_iota(jnp.int32, (tokens, tokens), 0) <= lax.broadcasted_iota(
+        jnp.int32, (tokens, tokens), 1
+    )
     for scan in (b_scan, c_scan):
-        scan.own[heads * rows :] = jnp.zeros((spare, 8, LANES), F32)
+        scan.own[...] = jnp.zeros(scan.own.shape, F32)
     for scan in (n_scan, m_scan):
         scan.own[...] = jnp.zeros(scan.own.shape, F32)
-        scan.total[...] = jnp.zeros(scan.own.shape, F32)
+        scan.total[...] = jnp.zeros(scan.total.shape, F32)
+        scan.flat[...] = jnp.zeros(scan.flat.shape, F32)
+    den_s[...] = jnp.ones(den_s.shape, F32)
+    c_s[...] = jnp.zeros(c_s.shape, F32)
 
     def tiles(h):
-        return slice(h * rows, (h + 1) * rows)
-
-    def columns(h):
+        return slice(h * tall, (h + 1) * tall)
+
+    def rows(h):
         return slice(h * width, (h + 1) * width)
 
     loads[1].wait()
-    for h in range(heads):
-        b_s[h, :, :width] = jnp.maximum(k_v[:, columns(h)], 0)
-    some = jnp.ones((8, tokens), BF16)
-    for h in range(heads):
-        n_scan.own[h : h + 1, :] = mm(some, b_s[h], NN)[0:1]
-    pl.semaphore_wait(barrier, len(at.plane) + len(at.column) + 1)
+    b_s[...] = jnp.maximum(k_v[...], 0)
+    some = jnp.ones((16, tokens), BF16)
+    for h in range(heads):
+        n_scan.own[h, :, :width] = mm(some, b_s[rows(h)], NT)[0:1]
+    pl.semaphore_wait(barrier, len(partners))
     n_scan.core_send()
 
     loads[2].wait()
     for h in range(heads):
-        v_s[h, :, :width] = v_v[:, columns(h)]
-    for h in range(heads):
-        b_scan.own[tiles(h)] = mm(b_s[h], v_s[h], TN)[:width].reshape(rows, 8, LANES)
+        state = mm(v_v[rows(h)], b_s[rows(h)], NT)
+        b_scan.own[tiles(h), :, :width] = state.reshape(tall, 8, width)
     b_scan.core_send()
     n_scan.plane_send()
 
     loads[0].wait()
-    for h in range(heads):
-        a_s[h, :, :width] = jnp.maximum(q_v[:, columns(h)], 0)
+    a_s[...] = jnp.maximum(q_v[...], 0)
     b_scan.plane_send()
 
     loads[5].wait()
-    n_scan.total[:heads, :width] = nm_v[...]
     loads[7].wait()
-    m_scan.total[:heads, :width] = gn_v[...]
-
-    loads[3].wait()
-    for h in range(heads):
-        g_s[h, :, :width] = g_v[:, columns(h)]
-    for h in range(heads):
-        scores = jnp.where(lower, mm(a_s[h], b_s[h], NT), 0.0)
-        den_s[h] = jnp.broadcast_to(1.0 + jnp.sum(scores, axis=1, keepdims=True), (tokens, LANES))
-        num_s[h] = mm(scores.astype(BF16), v_s[h], NN)
-        pt_s[h] = jnp.where(upper, mm(b_s[h], a_s[h], NT), 0.0).astype(BF16)
+    for h in range(heads):
+        n_scan.total[h, :, :width] = nm_v[h : h + 1]
+        m_scan.total[h, :, :width] = gn_v[h : h + 1]
+    for h in range(heads):
+        scores = jnp.where(upper, mm(b_s[rows(h)], a_s[rows(h)], TN), 0.0)
+        den_s[h : h + 1] = 1.0 + jnp.sum(scores, axis=0, keepdims=True)
+        pt_s[h] = scores.astype(BF16)
+    for h in range(heads):
+        num_s[rows(h)] = mm(v_v[rows(h)], pt_s[h], NN)
     n_scan.column_send()
 
     loads[4].wait()
@@ -361,98 +348,96 @@
     for init, state in ((init_s, st_v), (init_r, gs_v)):
         init[...] = jnp.zeros(init.shape, F32)
         for h in range(heads):
-            init[tiles(h), :, :width] = state[h].reshape(rows, 8, width)
+            init[tiles(h), :, :width] = state[h].T.reshape(tall, 8, width)
     b_scan.core_rest()
-    init_s[...] = init_s[...] + flag(at.c == 1) * b_scan.other[: heads * rows]
-
+    init_s[...] = init_s[...] + flag(at.c == 1) * b_scan.other[: heads * tall]
+    loads[3].wait()
     b_scan.column_send()
 
     n_scan.finish()
-    for h in range(heads):
-        high, low = split(n_scan.total[h : h + 1, :])
-        both = mm(a_s[h], jnp.broadcast_to(high, (LANES, LANES)), NT) + mm(
-            a_s[h], jnp.broadcast_to(low, (LANES, LANES)), NT
-        )
-        inverse = 1.0 / (den_s[h] + both)
-        den_s[h] = inverse
-        ub_s[h], ul_s[h] = split(g_s[h].astype(F32) * inverse)
-    for h in range(heads):
-        c_scan.own[tiles(h)] = mm(a_s[h], ub_s[h], TN)[:width].reshape(rows, 8, LANES)
+    high, low = split(n_scan.flat[:, :width])
+    for h in range(heads):
+        both = mm(high, a_s[rows(h)], NN) + mm(low, a_s[rows(h)], NN)
+        den_s[h : h + 1] = den_s[h : h + 1] + both[h : h + 1]
+    den_s[...] = 1.0 / den_s[...]
+    for h in range(heads):
+        scaled = g_v[rows(h)].astype(F32) * den_s[h : h + 1]
+        ub_s[rows(h)], ul_s[rows(h)] = split(scaled)
+    for h in range(heads):
+        state = mm(ub_s[rows(h)], a_s[rows(h)], NT)
+        c_scan.own[tiles(h), :, :width] = state.reshape(tall, 8, width)
     c_scan.core_send()
     for h in range(heads):
-        vp_s[h] = mm(pt_s[h], ub_s[h], NN)
+        vp_s[rows(h)] = mm(ub_s[rows(h)], pt_s[h], NT)
     c_scan.plane_send()
     b_scan.back_send()
     c_scan.core_rest()
-    init_r[...] = init_r[...] + flag(at.c == 0) * c_scan.other[: heads * rows]
+    init_r[...] = init_r[...] + flag(at.c == 0) * c_scan.other[: heads * tall]
+    c_scan.column_send()
     b_scan.back_pass()
-    c_scan.column_send()
     b_scan.finish()
 
     for h in range(heads):
         state = (b_scan.result[tiles(h)] + init_s[tiles(h)]).reshape(width, LANES)
-        sh_s[h, :width, :], sl_s[h, :width, :] = split(state)
-    for h in range(heads):
-        numerator = mm(a_s[h], sh_s[h], NN) + mm(a_s[h], sl_s[h], NN) + num_s[h]
-        inverse = den_s[h]
-        scaled = g_s[h].astype(F32) * inverse
-        c = -jnp.sum(scaled * (numerator * inverse), axis=1, keepdims=True)
-        c_s[h] = jnp.broadcast_to(c, (tokens, LANES))
-        m_scan.own[h : h + 1, :] = jnp.sum(c * a_s[h].astype(F32), axis=0, keepdims=True)
+        sh_s[rows(h)], sl_s[rows(h)] = split(state)
+    for h in range(heads):
+        numerator = num_s[rows(h)] + mm(sh_s[rows(h), :width], a_s[rows(h)], NN)
+        numerator = numerator + mm(sl_s[rows(h), :width], a_s[rows(h)], NN)
+        inverse = den_s[h : h + 1]
+        scaled = g_v[rows(h)].astype(F32) * inverse
+        c_s[h : h + 1] = -jnp.sum(scaled * (numerator * inverse), axis=0, keepdims=True)
+    both = jnp.concatenate(split(c_s[...]), axis=0)
+    for h in range(heads):
+        part = mm(both, a_s[rows(h)], NT)
+        m_scan.own[h, :, :width] = part[h : h + 1] + part[16 + h : 17 + h]
     m_scan.core_send()
     m_scan.plane_send()
-
-    for h in range(heads):
-        high, low = split(c_s[h])
-        ua_s[h] = jnp.where(lane == width, high, jnp.where(lane == width + 1, low, ub_s[h]))
-    for h in range(heads):
-        mixed = jnp.where(lower, mm(ua_s[h], v_s[h], NT), 0.0).astype(BF16)
-        part = mm(ub_s[h], sh_s[h], NT) + mm(ub_s[h], sl_s[h], NT) + mm(ul_s[h], sh_s[h], NT)
-        part = part + c_s[h] * n_scan.total[h : h + 1, :] + mm(mixed, b_s[h], NN)
-        part = jnp.where(a_s[h] > 0, part, 0.0)
-        dq_v[:, columns(h)] = part[:, :width].astype(BF16)
-        turned = jnp.where(upper, mm(v_s[h], ua_s[h], NT), 0.0).astype(BF16)
-        kp_s[h] = mm(turned, a_s[h], NN)
-    stores = [
-        pltpu.make_async_copy(src, dst, store_s.at[i])
-        for i, (src, dst) in enumerate(zip((dq_v, dk_v, dv_v), hbm_out))
-    ]
-    stores[0].start()
     c_scan.back_send()
+
+    turned = n_scan.flat[...].T
+    for h in range(heads):
+        here = rows(h)
+        c = c_s[h : h + 1]
+        mixed = jnp.where(upper, mm(v_v[here], ub_s[here], TN) + c, 0.0).astype(BF16)
+        high, low = sh_s[here, :width], sl_s[here, :width]
+        part = mm(high, ub_s[here], TN) + mm(low, ub_s[here], TN) + mm(high, ul_s[here], TN)
+        part = part + turned[:width, h : h + 1] * c + mm(b_s[here], mixed, NN)
+        dq_v[here] = jnp.where(a_s[here] > 0, part, 0.0).astype(BF16)
+        kp_s[here] = mm(a_s[here], mixed, NT)
     m_scan.column_send()
     c_scan.back_pass()
     c_scan.finish()
 
     for h in range(heads):
         state = (c_scan.result[tiles(h)] + init_r[tiles(h)]).reshape(width, LANES)
-        rh_s[h, :width, :], rl_s[h, :width, :] = split(state)
-    for h in range(heads):
-        part = vp_s[h] + mm(b_s[h], rh_s[h], NN) + mm(b_s[h], rl_s[h], NN)
-        dv_v[:, columns(h)] = part[:, :width].astype(BF16)
-    stores[2].start()
-    for h in range(heads):
-        kp_s[h] = kp_s[h] + mm(v_s[h], rh_s[h], NT) + mm(v_s[h], rl_s[h], NT)
+        sh_s[rows(h)], sl_s[rows(h)] = split(state)
+    for h in range(heads):
+        here = rows(h)
+        high, low = sh_s[here, :width], sl_s[here, :width]
+        part = vp_s[here] + mm(high, b_s[here], NN) + mm(low, b_s[here], NN)
+        dv_v[here] = part.astype(BF16)
+        kp_s[here] = kp_s[here] + mm(high, v_v[here], TN) + mm(low, v_v[here], TN)
     m_scan.finish()
-    for h in range(heads):
-        part = jnp.where(b_s[h] > 0, kp_s[h] + m_scan.total[h : h + 1, :], 0.0)
-        dk_v[:, columns(h)] = part[:, :width].astype(BF16)
-    stores[1].start()
+    turned = m_scan.flat[...].T
+    for h in range(heads):
+        here = rows(h)
+        part = jnp.where(b_s[here] > 0, kp_s[here] + turned[:width, h : h + 1], 0.0)
+        dk_v[here] = part.astype(BF16)
     for scan in (n_scan, b_scan, m_scan, c_scan):
         scan.drain()
-    for copy in stores:
-        copy.wait()
-
-
-def small_scratch(groups, chips):
-    one = pltpu.VMEM((16, LANES), F32)
+
+
+def small_scratch(groups, chips, heads):
+    one = (heads, 1, LANES)
     sem = pltpu.SemaphoreType.DMA
     return [
-        one,
-        one,
-        one,
-        pltpu.VMEM((chips, 16, LANES), F32),
-        pltpu.VMEM((groups, 16, LANES), F32),
-        one,
+        pltpu.VMEM(one, F32),
+        pltpu.VMEM(one, F32),
+        pltpu.VMEM(one, F32),
+        pltpu.VMEM((chips, *one), F32),
+        pltpu.VMEM((groups, *one), F32),
+        pltpu.VMEM(one, F32),
+        pltpu.VMEM((16, LANES), F32),
         sem((2, 1)),
         sem((2, chips - 1)),
         sem((2, groups - 1)),
@@ -479,33 +464,53 @@
     ]
 
 
+def place(*refs):
+    sems = refs[6]
+    copies = [pltpu.make_async_copy(refs[i], refs[3 + i], sems.at[i]) for i in range(3)]
+    for copy in copies:
+        copy.start()
+    for copy in copies:
+        copy.wait()
+
+
 def per_device(groups, chips, *args):
-    tokens, columns = args[0].shape
+    args = [x.T for x in args[:4]] + list(args[4:])
+    columns, tokens = args[0].shape
     heads, width = args[4].shape[:2]
     share = -(-(heads * width // 8) // (2 * chips))
-    token = pltpu.VMEM((tokens, columns), BF16)
+    token = pltpu.VMEM((columns, tokens), BF16)
+    wide = pltpu.VMEM((columns, tokens), F32)
     state = pltpu.VMEM((heads, width, width), F32)
     norm = pltpu.VMEM((heads, width), F32)
-    low = pltpu.VMEM((heads, tokens, LANES), BF16)
-    square = pltpu.VMEM((heads, LANES, LANES), BF16)
-    wide = pltpu.VMEM((heads, tokens, LANES), F32)
+    one = pltpu.VMEM((16, tokens), F32)
     init = pltpu.VMEM((heads * width // 8, 8, LANES), F32)
     sem = pltpu.SemaphoreType.DMA
-    scratch = [token] * 4 + [state, norm, state, norm] + [token] * 3
-    scratch += [low] * 7 + [square] + [square] * 4
-    scratch += [wide] * 5 + [init] * 2 + [sem((8,)), sem((3,))]
-    scratch += small_scratch(groups, chips) * 2 + large_scratch(groups, chips, share) * 2
-    return pl.pallas_call(
+    scratch = [token] * 4 + [state, norm, state, norm]
+    scratch += [token] * 4 + [pltpu.VMEM((columns, LANES), BF16)] * 2
+    scratch += [pltpu.VMEM((heads, tokens, tokens), BF16)]
+    scratch += [wide] * 3 + [one] * 2 + [init] * 2 + [sem((8,))]
+    scratch += small_scratch(groups, chips, heads) * 2 + large_scratch(groups, chips, share) * 2
+    outs = pl.pallas_call(
         functools.partial(kernel, groups, chips, heads, width, share),
-        out_shape=[jax.ShapeDtypeStruct((tokens, columns), BF16)] * 3,
+        out_shape=[pltpu.VMEM((columns, tokens), BF16)] * 3,
         in_specs=[pl.BlockSpec(memory_space=pl.ANY)] * 8,
-        out_specs=[pl.BlockSpec(memory_space=pl.ANY)] * 3,
+        out_specs=[pl.BlockSpec(memory_space=pltpu.VMEM)] * 3,
         scratch_shapes=scratch,
         compiler_params=pltpu.CompilerParams(
-            collective_id=0, has_side_effects=True, vmem_limit_bytes=40 * 2**20
+            collective_id=0, has_side_effects=True, vmem_limit_bytes=60 * 2**20
         ),
         name="scan_kernel",
     )(*args)
+    outs = pl.pallas_call(
+        place,
+        out_shape=[jax.ShapeDtypeStruct((columns, tokens), BF16)] * 3,
+        in_specs=[pl.BlockSpec(memory_space=pl.ANY)] * 3,
+        out_specs=[pl.BlockSpec(memory_space=pl.ANY)] * 3,
+        scratch_shapes=[sem((3,))],
+        compiler_params=pltpu.CompilerParams(vmem_limit_bytes=2**20),
+        name="place_outputs",
+    )(*outs)
+    return tuple(x.T for x in outs)
 
 
 def solution(mesh):

time: 59 us -> 50.4 us (0.85)
  local copies, waits for them, and re-layouts: 7.48 us -> 0 us
  Pallas kernels: 50.6 us -> 49.7 us
    unnamed x18 -> x0, local copies, waits for them, and re-layouts: 4.8 us -> none
    pallas_call x3 -> x0, local copies, waits for them, and re-layouts: 2.67 us -> none  [per_device(): pl.pallas_call(functools.partial(kernel, groups, chips, heads, width, sha...]
    pallas_call x1, Pallas kernels: 50.6 us -> 48.7 us  [per_device(): pl.pallas_call(functools.partial(kernel, groups, chips, heads, width, sha...]
    pallas_call x0 -> x1, Pallas kernels: none -> 0.96 us  [per_device(): pl.pallas_call(place, out_shape=[jax.ShapeDtypeStruct((columns, tokens),...]
where the time goes in v2:
time: 50.4 us; the launch traced here: 50.3 us
  Pallas kernels  49.7 us (99%)
  between operations  0.64 us (1%)
    pallas_call x1, Pallas kernels, per_device(): pl.pallas_call(functools.partial(kernel, groups, chips, heads, width, sha...  48.7 us

profile of v2, /device:TPU:1, one launch (start us, length us, event | category | flops | bytes accessed | tf_op | source)
XLA Modules:
  0.0 50.3 jit_solution(16849863322622604576)
XLA Ops:
  0.6 48.7 %scan_kernel.1 = (bf16[1232,128]{1,0:T(8,128)(2,1)S(1)}, bf16[1232,128]{1,0:T(8,128)(2,1)S(1)}, bf16[1232,128]{1,0:T(8,128)(2,1)S(1)}) custom-call(bf16[1232,128]{1,0:T(8,128)(2,1)} %bitcast.7, bf16[1232,128]{1,0:T(8,128)(2,1)} %bitcast.8, bf16[1232,128]{1,0:T(8,128)(2,1)} %bitcast.9, bf16[1232,128]{1,0:T(8,128)(2,1)} %bitcast.10, f32[11,112,112]{2,1,0:T(8,128)} %refs_4_.1, ...), custom_call_target="tpu_custom_call" | custom-call | tf_op jit(solution)/shard_map/scan_kernel/pallas_call | solution.py:493
  49.4 1.0 %place_outputs.1 = (bf16[1232,128]{1,0:T(8,128)(2,1)}, bf16[1232,128]{1,0:T(8,128)(2,1)}, bf16[1232,128]{1,0:T(8,128)(2,1)}) custom-call(bf16[1232,128]{1,0:T(8,128)(2,1)S(1)} %get-tuple-element.9.refs_0_, bf16[1232,128]{1,0:T(8,128)(2,1)S(1)} %get-tuple-element.10.refs_1_, bf16[1232,128]{1,0:T(8,128)(2,1)S(1)} %get-tuple-element.11.refs_2_), custom_call_target="tpu_custom_call" | custom-call | tf_op jit(solution)/shard_map/place_outputs/pallas_call | solution.py:504

commit v3 on v2

--- a/solution.py
+++ b/solution.py
@@ -77,204 +77,215 @@
     return condition.astype(jnp.int32).astype(F32)
 
 
+def arrived(ref, sem):
+    pltpu.make_async_copy(ref, ref, sem).wait()
+
+
+def z_send(at, later, start):
+    for k in reversed(range(len(at.column))):
+        offset = at.column[k]
+        target = at.z - offset if later else at.z + offset
+        inside = target >= 0 if later else target < at.groups
+
+        @pl.when(inside)
+        def _():
+            start(target)
+
+
+def z_arrived(at, below, view, sem):
+    for n in range(1, at.groups):
+
+        @pl.when(at.z == (n if below else at.groups - 1 - n))
+        def _():
+            arrived(view(n), sem)
+
+
 class SmallScan:
     def __init__(self, at, later, refs):
         self.at, self.later = at, later
         self.own, self.other, self.chip, self.plane, self.column, self.total, self.flat = refs[:7]
-        self.core_s, self.plane_s, self.column_s = refs[7:]
-        self.sent = []
-
-    def start(self, copy):
-        copy.start()
-        self.sent.append(copy)
-
-    def core_copy(self):
-        sems = self.core_s
-        return remote(self.own, self.other, sems.at[0, 0], sems.at[1, 0], self.at.core_id())
+        self.sems = refs[7]
+        self.reached = (lambda i, me: i > me) if later else (lambda i, me: i < me)
 
     def core_send(self):
-        self.start(self.core_copy())
-
-    def plane_copy(self, k, slot, device):
-        sems = self.plane_s
-        return remote(self.chip, self.plane.at[slot], sems.at[0, k], sems.at[1, k], device)
+        sems = self.sems
+        remote(self.own, self.other, sems.at[0], sems.at[1], self.at.core_id()).start()
 
     def plane_send(self):
-        at = self.at
-        self.core_copy().wait_recv()
+        at, sems = self.at, self.sems
+        arrived(self.other, sems.at[1])
         both = self.own[...] + self.other[...]
         self.chip[...] = both
         for k in reversed(range(len(at.plane))):
-            self.start(self.plane_copy(k, at.p, at.chip_id(at.plane_to(k))))
+            device = at.chip_id(at.plane_to(k))
+            remote(self.chip, self.plane.at[at.p], sems.at[2], sems.at[3], device).start()
         self.plane[at.p] = both
 
-    def column_copy(self, k, slot, device):
-        sems = self.column_s
-        return remote(
-            self.column.at[self.at.z], self.column.at[slot], sems.at[0, k], sems.at[1, k], device
-        )
-
     def column_send(self):
-        at = self.at
-        for k in range(len(at.plane)):
-            source = at.plane_from(k)
-            self.plane_copy(k, source, at.chip_id(source)).wait_recv()
+        at, sems = self.at, self.sems
+        arrived(self.plane.at[: at.chips - 1], sems.at[3])
         everything = self.plane[0]
         for p in range(1, at.chips):
             everything = everything + self.plane[p]
         self.column[at.z] = everything
-        for k in reversed(range(len(at.column))):
-            self.start(self.column_copy(k, at.z, at.z_id(at.z_to(k))))
-        reached = (lambda i, me: i > me) if self.later else (lambda i, me: i < me)
+        mine = self.column.at[at.z]
+        z_send(
+            at,
+            self.later,
+            lambda z: remote(mine, mine, sems.at[4], sems.at[5], at.z_id(z)).start(),
+        )
         near = flag(at.c == (0 if self.later else 1)) * self.other[...]
         for p in range(at.chips):
-            near = near + flag(reached(p, at.p)) * self.plane[p]
+            near = near + flag(self.reached(p, at.p)) * self.plane[p]
         self.total[...] = self.total[...] + near
 
     def finish(self):
         at = self.at
-        for k in range(len(at.column)):
-            source = at.z_from(k)
-            self.column_copy(k, source, at.z_id(source)).wait_recv()
-        reached = (lambda i, me: i > me) if self.later else (lambda i, me: i < me)
-        far = flag(reached(0, at.z)) * self.column[0]
+        z_arrived(at, not self.later, lambda n: self.column.at[:n], self.sems.at[5])
+        far = jnp.where(self.reached(0, at.z), self.column[0], 0.0)
         for z in range(1, at.groups):
-            far = far + flag(reached(z, at.z)) * self.column[z]
+            far = far + jnp.where(self.reached(z, at.z), self.column[z], 0.0)
         self.total[...] = self.total[...] + far
         for h in range(self.total.shape[0]):
             self.flat[h : h + 1, :] = self.total[h]
 
     def drain(self):
-        for copy in self.sent:
-            copy.wait_send()
+        at, sems = self.at, self.sems
+        arrived(self.own, sems.at[0])
+        arrived(self.plane.at[: at.chips - 1], sems.at[2])
+        z_arrived(at, self.later, lambda n: self.column.at[:n], sems.at[4])
 
 
 class LargeScan:
-    def __init__(self, at, later, share, refs):
-        self.at, self.later, self.share = at, later, share
+    def __init__(self, at, later, share, chunks, refs):
+        self.at, self.later, self.share, self.chunks = at, later, share, chunks
         self.own, self.other, self.chip, self.plane, self.column, self.back, self.result = refs[:7]
-        self.core_s, self.plane_s, self.column_s, self.back_s, self.pass_s = refs[7:]
+        self.core_s, self.chunk_s, self.back_s = refs[7:]
         self.half = share * at.chips
-        self.sent = []
-
-    def start(self, copy):
-        copy.start()
-        self.sent.append(copy)
-
-    def piece(self, p):
-        return pl.ds((self.at.c * self.at.chips + p) * self.share, self.share)
+        self.reached = (lambda i, me: i > me) if later else (lambda i, me: i < me)
+
+    def piece(self, core, p, chunk=None):
+        first, count = (0, self.share) if chunk is None else self.chunks[chunk]
+        return pl.ds((core * self.at.chips + p) * self.share + first, count)
+
+    def part(self, chunk):
+        first, count = self.chunks[chunk]
+        return pl.ds(first, count)
 
     def core_copy(self, k, core):
-        part = pl.ds(core * self.half, self.half)
+        half = pl.ds(core * self.half, self.half)
         sems = self.core_s
         return remote(
-            self.own.at[part], self.other.at[part], sems.at[0, k], sems.at[1, k], self.at.core_id()
+            self.own.at[half], self.other.at[half], sems.at[0, k], sems.at[1, k], self.at.core_id()
         )
 
     def core_send(self):
-        self.start(self.core_copy(0, 1 - self.at.c))
-        self.start(self.core_copy(1, self.at.c))
-
-    def plane_copy(self, k, src, slot, device):
-        sems = self.plane_s
-        return remote(self.chip.at[src], self.plane.at[slot], sems.at[0, k], sems.at[1, k], device)
+        self.core_copy(0, 1 - self.at.c).start()
+        self.core_copy(1, self.at.c).start()
+
+    def core_rest(self):
+        self.core_copy(1, 1 - self.at.c).wait_recv()
 
     def plane_send(self):
         at = self.at
         self.core_copy(0, at.c).wait_recv()
-        for k in reversed(range(len(at.plane))):
-            target = at.plane_to(k)
-            part = self.piece(target)
-            self.chip[target] = self.own[part] + self.other[part]
-            self.start(self.plane_copy(k, target, at.p, at.chip_id(target)))
-        part = self.piece(at.p)
-        self.plane[at.p] = self.own[part] + self.other[part]
-
-    def column_copy(self, k, slot, device):
-        sems = self.column_s
-        return remote(
-            self.column.at[self.at.z], self.column.at[slot], sems.at[0, k], sems.at[1, k], device
-        )
-
-    def column_send(self):
+        for i in range(len(self.chunks)):
+            part, sems = self.part(i), self.chunk_s.at[i]
+            for k in reversed(range(len(at.plane))):
+                target = at.plane_to(k)
+                piece = self.piece(at.c, target, i)
+                self.chip[target, part] = self.own[piece] + self.other[piece]
+                remote(
+                    self.chip.at[target, part],
+                    self.plane.at[at.p, part],
+                    sems.at[0],
+                    sems.at[1],
+                    at.chip_id(target),
+                ).start()
+        piece = self.piece(at.c, at.p)
+        self.plane[at.p] = self.own[piece] + self.other[piece]
+
+    def column_send(self, i):
         at = self.at
-        for k in range(len(at.plane)):
-            source = at.plane_from(k)
-            self.plane_copy(k, source, source, at.chip_id(source)).wait_recv()
+        part, sems = self.part(i), self.chunk_s.at[i]
+        arrived(self.plane.at[: at.chips - 1, part], sems.at[1])
         order = list(range(at.chips))
         if self.later:
             order.reverse()
-        running = jnp.zeros(self.column.shape[1:], F32)
+        running = jnp.zeros((self.chunks[i][1], *self.column.shape[2:]), F32)
         for p in order:
-            self.back[p] = running
-            running = running + self.plane[p]
-        self.column[at.z] = running
-        for k in reversed(range(len(at.column))):
-            self.start(self.column_copy(k, at.z, at.z_id(at.z_to(k))))
-
-    def back_copy(self, k, src, owner, device):
-        sems = self.back_s
-        return remote(
-            self.back.at[src], self.result.at[self.piece(owner)], sems.at[0, k], sems.at[1, k], device
+            self.back[p, part] = running
+            running = running + self.plane[p, part]
+        self.column[at.z, part] = running
+        mine = self.column.at[at.z, part]
+        z_send(
+            at,
+            self.later,
+            lambda z: remote(mine, mine, sems.at[2], sems.at[3], at.z_id(z)).start(),
         )
 
-    def pass_copy(self, k, core, owner):
-        part = pl.ds((core * self.at.chips + owner) * self.share, self.share)
-        sems = self.pass_s
-        return remote(
-            self.result.at[part], self.result.at[part], sems.at[0, k], sems.at[1, k], self.at.core_id()
-        )
-
-    def back_send(self):
+    def pass_on(self, owner):
+        mine = self.result.at[self.piece(self.at.c, owner)]
+        remote(mine, mine, self.core_s.at[0, 2], self.core_s.at[1, 2], self.at.core_id()).start()
+
+    def back_send(self, i):
         at = self.at
-        for k in range(len(at.column)):
-            source = at.z_from(k)
-            self.column_copy(k, source, at.z_id(source)).wait_recv()
-        reached = (lambda i, me: i > me) if self.later else (lambda i, me: i < me)
-        far = flag(reached(0, at.z)) * self.column[0]
+        part, sems = self.part(i), self.chunk_s.at[i]
+        z_arrived(at, not self.later, lambda n: self.column.at[:n, part], sems.at[3])
+        far = jnp.where(self.reached(0, at.z), self.column[0, part], 0.0)
         for z in range(1, at.groups):
-            far = far + flag(reached(z, at.z)) * self.column[z]
+            far = far + jnp.where(self.reached(z, at.z), self.column[z, part], 0.0)
         for k in reversed(range(len(at.plane))):
             target = at.plane_to(k)
-            self.back[target] = self.back[target] + far
-            self.start(self.back_copy(k, target, at.p, at.chip_id(target)))
-        self.result[self.piece(at.p)] = self.back[at.p] + far
-        self.start(self.pass_copy(len(at.plane), at.c, at.p))
+            self.back[target, part] = self.back[target, part] + far
+            remote(
+                self.back.at[target, part],
+                self.result.at[self.piece(at.c, at.p, i)],
+                sems.at[4],
+                self.back_s.at[k],
+                at.chip_id(target),
+            ).start()
+        self.result[self.piece(at.c, at.p, i)] = self.back[at.p, part] + far
+        if i == len(self.chunks) - 1:
+            self.pass_on(at.p)
 
     def back_pass(self):
         at = self.at
         for k in range(len(at.plane)):
             source = at.plane_from(k)
-            self.back_copy(k, source, source, at.chip_id(source)).wait_recv()
-            self.start(self.pass_copy(k, at.c, source))
-
-    def core_rest(self):
-        self.core_copy(1, 1 - self.at.c).wait_recv()
+            arrived(self.result.at[self.piece(at.c, source)], self.back_s.at[k])
+            self.pass_on(source)
 
     def finish(self):
+        half = pl.ds((1 - self.at.c) * self.half, self.half)
+        arrived(self.result.at[half], self.core_s.at[1, 2])
+
+    def drain(self):
         at = self.at
-        for k in range(len(at.plane)):
-            self.pass_copy(k, 1 - at.c, at.plane_from(k)).wait_recv()
-        self.pass_copy(len(at.plane), 1 - at.c, at.p).wait_recv()
-
-    def drain(self):
-        for copy in self.sent:
-            copy.wait_send()
-
-
-def kernel(groups, chips, heads, width, share, *refs):
+        half = pl.ds(0, self.half)
+        for k in range(2):
+            arrived(self.own.at[half], self.core_s.at[0, k])
+        arrived(self.result.at[half], self.core_s.at[0, 2])
+        for i in range(len(self.chunks)):
+            part, sems = self.part(i), self.chunk_s.at[i]
+            arrived(self.plane.at[: at.chips - 1, part], sems.at[0])
+            z_arrived(at, self.later, lambda n: self.column.at[:n, part], sems.at[2])
+            arrived(self.plane.at[: at.chips - 1, part], sems.at[4])
+
+
+def kernel(groups, chips, heads, width, share, chunks, *refs):
     hbm_in, (dq_v, dk_v, dv_v), refs = refs[:8], refs[8:11], refs[11:]
     q_v, k_v, v_v, g_v, st_v, nm_v, gs_v, gn_v = refs[:8]
     a_s, b_s, ub_s, ul_s, sh_s, sl_s, pt_s = refs[8:15]
     num_s, kp_s, vp_s, den_s, c_s, init_s, init_r = refs[15:22]
     load_s = refs[22]
-    small = refs[23:43]
-    large = refs[43:]
+    small = refs[23:39]
+    large = refs[39:]
     at = Place(groups, chips)
-    n_scan = SmallScan(at, False, small[:10])
-    m_scan = SmallScan(at, True, small[10:])
-    b_scan = LargeScan(at, False, share, large[:12])
-    c_scan = LargeScan(at, True, share, large[12:])
+    n_scan = SmallScan(at, False, small[:8])
+    m_scan = SmallScan(at, True, small[8:])
+    b_scan = LargeScan(at, False, share, chunks, large[:10])
+    c_scan = LargeScan(at, True, share, chunks, large[10:])
     tokens = k_v.shape[1]
     tall = width // 8
 
@@ -352,7 +363,8 @@
     b_scan.core_rest()
     init_s[...] = init_s[...] + flag(at.c == 1) * b_scan.other[: heads * tall]
     loads[3].wait()
-    b_scan.column_send()
+    for i in range(len(chunks)):
+        b_scan.column_send(i)
 
     n_scan.finish()
     high, low = split(n_scan.flat[:, :width])
@@ -370,10 +382,12 @@
     for h in range(heads):
         vp_s[rows(h)] = mm(ub_s[rows(h)], pt_s[h], NT)
     c_scan.plane_send()
-    b_scan.back_send()
+    for i in range(len(chunks)):
+        b_scan.back_send(i)
     c_scan.core_rest()
     init_r[...] = init_r[...] + flag(at.c == 0) * c_scan.other[: heads * tall]
-    c_scan.column_send()
+    for i in range(len(chunks)):
+        c_scan.column_send(i)
     b_scan.back_pass()
     b_scan.finish()
 
@@ -392,7 +406,8 @@
         m_scan.own[h, :, :width] = part[h : h + 1] + part[16 + h : 17 + h]
     m_scan.core_send()
     m_scan.plane_send()
-    c_scan.back_send()
+    for i in range(len(chunks)):
+        c_scan.back_send(i)
 
     turned = n_scan.flat[...].T
     for h in range(heads):
@@ -429,7 +444,6 @@
 
 def small_scratch(groups, chips, heads):
     one = (heads, 1, LANES)
-    sem = pltpu.SemaphoreType.DMA
     return [
         pltpu.VMEM(one, F32),
         pltpu.VMEM(one, F32),
@@ -438,13 +452,11 @@
         pltpu.VMEM((groups, *one), F32),
         pltpu.VMEM(one, F32),
         pltpu.VMEM((16, LANES), F32),
-        sem((2, 1)),
-        sem((2, chips - 1)),
-        sem((2, groups - 1)),
+        pltpu.SemaphoreType.DMA((6,)),
     ]
 
 
-def large_scratch(groups, chips, share):
+def large_scratch(groups, chips, share, chunks):
     whole = pltpu.VMEM((2 * chips * share, 8, LANES), F32)
     plane = pltpu.VMEM((chips, share, 8, LANES), F32)
     sem = pltpu.SemaphoreType.DMA
@@ -456,11 +468,9 @@
         pltpu.VMEM((groups, share, 8, LANES), F32),
         plane,
         whole,
-        sem((2, 2)),
-        sem((2, chips - 1)),
-        sem((2, groups - 1)),
-        sem((2, chips - 1)),
-        sem((2, chips)),
+        sem((2, 3)),
+        sem((len(chunks), 5)),
+        sem((chips - 1,)),
     ]
 
 
@@ -478,6 +488,7 @@
     columns, tokens = args[0].shape
     heads, width = args[4].shape[:2]
     share = -(-(heads * width // 8) // (2 * chips))
+    chunks = ((0, share),)
     token = pltpu.VMEM((columns, tokens), BF16)
     wide = pltpu.VMEM((columns, tokens), F32)
     state = pltpu.VMEM((heads, width, width), F32)
@@ -489,9 +500,9 @@
     scratch += [token] * 4 + [pltpu.VMEM((columns, LANES), BF16)] * 2
     scratch += [pltpu.VMEM((heads, tokens, tokens), BF16)]
     scratch += [wide] * 3 + [one] * 2 + [init] * 2 + [sem((8,))]
-    scratch += small_scratch(groups, chips, heads) * 2 + large_scratch(groups, chips, share) * 2
+    scratch += small_scratch(groups, chips, heads) * 2 + large_scratch(groups, chips, share, chunks) * 2
     outs = pl.pallas_call(
-        functools.partial(kernel, groups, chips, heads, width, share),
+        functools.partial(kernel, groups, chips, heads, width, share, chunks),
         out_shape=[pltpu.VMEM((columns, tokens), BF16)] * 3,
         in_specs=[pl.BlockSpec(memory_space=pl.ANY)] * 8,
         out_specs=[pl.BlockSpec(memory_space=pltpu.VMEM)] * 3,

time: 50.4 us -> 46.3 us (0.919)
  Pallas kernels: 49.7 us -> 45.5 us
    pallas_call x1, Pallas kernels: 48.7 us -> 44.6 us  [per_device(): pl.pallas_call(functools.partial(kernel, groups, chips, heads, width, sha...]
where the time goes in v3:
time: 46.3 us; the launch traced here: 46.2 us
  Pallas kernels  45.5 us (98%)
  between operations  0.64 us (1%)
    pallas_call x1, Pallas kernels, per_device(): pl.pallas_call(functools.partial(kernel, groups, chips, heads, width, sha...  44.6 us
    pallas_call x1, Pallas kernels, per_device(): pl.pallas_call(place, out_shape=[jax.ShapeDtypeStruct((columns, tokens),...  0.96 us

profile of v3, /device:TPU:1, one launch (start us, length us, event | category | flops | bytes accessed | tf_op | source)
XLA Modules:
  0.0 46.2 jit_solution(12911731350365343393)
XLA Ops:
  0.6 44.6 %scan_kernel.1 = (bf16[1232,128]{1,0:T(8,128)(2,1)S(1)}, bf16[1232,128]{1,0:T(8,128)(2,1)S(1)}, bf16[1232,128]{1,0:T(8,128)(2,1)S(1)}) custom-call(bf16[1232,128]{1,0:T(8,128)(2,1)} %bitcast.7, bf16[1232,128]{1,0:T(8,128)(2,1)} %bitcast.8, bf16[1232,128]{1,0:T(8,128)(2,1)} %bitcast.9, bf16[1232,128]{1,0:T(8,128)(2,1)} %bitcast.10, f32[11,112,112]{2,1,0:T(8,128)} %refs_4_.1, ...), custom_call_target="tpu_custom_call" | custom-call | tf_op jit(solution)/shard_map/scan_kernel/pallas_call | solution.py:504
  45.2 1.0 %place_outputs.1 = (bf16[1232,128]{1,0:T(8,128)(2,1)}, bf16[1232,128]{1,0:T(8,128)(2,1)}, bf16[1232,128]{1,0:T(8,128)(2,1)}) custom-call(bf16[1232,128]{1,0:T(8,128)(2,1)S(1)} %get-tuple-element.9.refs_0_, bf16[1232,128]{1,0:T(8,128)(2,1)S(1)} %get-tuple-element.10.refs_1_, bf16[1232,128]{1,0:T(8,128)(2,1)S(1)} %get-tuple-element.11.refs_2_), custom_call_target="tpu_custom_call" | custom-call | tf_op jit(solution)/shard_map/place_outputs/pallas_call | solution.py:515

commit v4 on v3

--- a/solution.py
+++ b/solution.py
@@ -181,7 +181,6 @@
 
     def core_send(self):
         self.core_copy(0, 1 - self.at.c).start()
-        self.core_copy(1, self.at.c).start()
 
     def core_rest(self):
         self.core_copy(1, 1 - self.at.c).wait_recv()
@@ -202,6 +201,7 @@
                     sems.at[1],
                     at.chip_id(target),
                 ).start()
+        self.core_copy(1, at.c).start()
         piece = self.piece(at.c, at.p)
         self.plane[at.p] = self.own[piece] + self.other[piece]
 
@@ -334,8 +334,8 @@
     for h in range(heads):
         state = mm(v_v[rows(h)], b_s[rows(h)], NT)
         b_scan.own[tiles(h), :, :width] = state.reshape(tall, 8, width)
+    n_scan.plane_send()
     b_scan.core_send()
-    n_scan.plane_send()
 
     loads[0].wait()
     a_s[...] = jnp.maximum(q_v[...], 0)
@@ -363,8 +363,6 @@
     b_scan.core_rest()
     init_s[...] = init_s[...] + flag(at.c == 1) * b_scan.other[: heads * tall]
     loads[3].wait()
-    for i in range(len(chunks)):
-        b_scan.column_send(i)
 
     n_scan.finish()
     high, low = split(n_scan.flat[:, :width])
@@ -379,6 +377,8 @@
         state = mm(ub_s[rows(h)], a_s[rows(h)], NT)
         c_scan.own[tiles(h), :, :width] = state.reshape(tall, 8, width)
     c_scan.core_send()
+    for i in range(len(chunks)):
+        b_scan.column_send(i)
     for h in range(heads):
         vp_s[rows(h)] = mm(ub_s[rows(h)], pt_s[h], NT)
     c_scan.plane_send()

time: 46.3 us -> 46 us (level)
  Pallas kernels: 45.5 us -> 44.8 us
    pallas_call x1, Pallas kernels: 44.6 us -> 43.9 us  [per_device(): pl.pallas_call(functools.partial(kernel, groups, chips, heads, width, sha...]
where the time goes in v4:
time: 46 us; the launch traced here: 45.5 us
  Pallas kernels  44.8 us (97%)
  between operations  0.64 us (1%)
    pallas_call x1, Pallas kernels, per_device(): pl.pallas_call(functools.partial(kernel, groups, chips, heads, width, sha...  43.9 us
    pallas_call x1, Pallas kernels, per_device(): pl.pallas_call(place, out_shape=[jax.ShapeDtypeStruct((columns, tokens),...  0.96 us

profile of v4, /device:TPU:1, one launch (start us, length us, event | category | flops | bytes accessed | tf_op | source)
XLA Modules:
  0.0 45.5 jit_solution(13787198213523326539)
XLA Ops:
  0.6 43.9 %scan_kernel.1 = (bf16[1232,128]{1,0:T(8,128)(2,1)S(1)}, bf16[1232,128]{1,0:T(8,128)(2,1)S(1)}, bf16[1232,128]{1,0:T(8,128)(2,1)S(1)}) custom-call(bf16[1232,128]{1,0:T(8,128)(2,1)} %bitcast.7, bf16[1232,128]{1,0:T(8,128)(2,1)} %bitcast.8, bf16[1232,128]{1,0:T(8,128)(2,1)} %bitcast.9, bf16[1232,128]{1,0:T(8,128)(2,1)} %bitcast.10, f32[11,112,112]{2,1,0:T(8,128)} %refs_4_.1, ...), custom_call_target="tpu_custom_call" | custom-call | tf_op jit(solution)/shard_map/scan_kernel/pallas_call | solution.py:504
  44.5 1.0 %place_outputs.1 = (bf16[1232,128]{1,0:T(8,128)(2,1)}, bf16[1232,128]{1,0:T(8,128)(2,1)}, bf16[1232,128]{1,0:T(8,128)(2,1)}) custom-call(bf16[1232,128]{1,0:T(8,128)(2,1)S(1)} %get-tuple-element.9.refs_0_, bf16[1232,128]{1,0:T(8,128)(2,1)S(1)} %get-tuple-element.10.refs_1_, bf16[1232,128]{1,0:T(8,128)(2,1)S(1)} %get-tuple-element.11.refs_2_), custom_call_target="tpu_custom_call" | custom-call | tf_op jit(solution)/shard_map/place_outputs/pallas_call | solution.py:515

commit v5 on v4

--- a/solution.py
+++ b/solution.py
@@ -37,6 +37,7 @@
         side = self.side
         offsets = [(dy, dx) for dy in range(side) for dx in range(side) if dy or dx]
         self.plane = sorted(offsets, key=lambda o: min(o[0], side - o[0]) + min(o[1], side - o[1]))
+        self.far_rows = sorted(range(side), key=lambda d: -min(d, side - d))
         self.column = sorted(range(1, groups), key=lambda d: min(d, groups - d))
 
     def chip(self, offset, sign):
@@ -224,10 +225,6 @@
             lambda z: remote(mine, mine, sems.at[2], sems.at[3], at.z_id(z)).start(),
         )
 
-    def pass_on(self, owner):
-        mine = self.result.at[self.piece(self.at.c, owner)]
-        remote(mine, mine, self.core_s.at[0, 2], self.core_s.at[1, 2], self.at.core_id()).start()
-
     def back_send(self, i):
         at = self.at
         part, sems = self.part(i), self.chunk_s.at[i]
@@ -242,19 +239,19 @@
                 self.back.at[target, part],
                 self.result.at[self.piece(at.c, at.p, i)],
                 sems.at[4],
-                self.back_s.at[k],
+                self.back_s.at[at.plane[k][0]],
                 at.chip_id(target),
             ).start()
         self.result[self.piece(at.c, at.p, i)] = self.back[at.p, part] + far
-        if i == len(self.chunks) - 1:
-            self.pass_on(at.p)
 
     def back_pass(self):
         at = self.at
-        for k in range(len(at.plane)):
-            source = at.plane_from(k)
-            arrived(self.result.at[self.piece(at.c, source)], self.back_s.at[k])
-            self.pass_on(source)
+        for dy in reversed(at.far_rows):
+            first = at.c * at.chips + (at.y + at.side - dy) % at.side * at.side
+            row = self.result.at[pl.ds(first * self.share, at.side * self.share)]
+            count = at.side if dy else at.side - 1
+            arrived(self.result.at[pl.ds(first * self.share, count * self.share)], self.back_s.at[dy])
+            remote(row, row, self.core_s.at[0, 2], self.core_s.at[1, 2], at.core_id()).start()
 
     def finish(self):
         half = pl.ds((1 - self.at.c) * self.half, self.half)
@@ -470,7 +467,7 @@
         whole,
         sem((2, 3)),
         sem((len(chunks), 5)),
-        sem((chips - 1,)),
+        sem((math.isqrt(chips),)),
     ]
 
 

time: 46 us -> 45.6 us (level)
  no operation moved by 1% of the time
where the time goes in v5:
time: 45.6 us; the launch traced here: 45.3 us
  Pallas kernels  44.7 us (98%)
  between operations  0.64 us (1%)
    pallas_call x1, Pallas kernels, per_device(): pl.pallas_call(functools.partial(kernel, groups, chips, heads, width, sha...  43.7 us
    pallas_call x1, Pallas kernels, per_device(): pl.pallas_call(place, out_shape=[jax.ShapeDtypeStruct((columns, tokens),...  0.96 us

profile of v5, /device:TPU:1, one launch (start us, length us, event | category | flops | bytes accessed | tf_op | source)
XLA Modules:
  0.0 45.3 jit_solution(6381197171222499267)
XLA Ops:
  0.6 43.7 %scan_kernel.1 = (bf16[1232,128]{1,0:T(8,128)(2,1)S(1)}, bf16[1232,128]{1,0:T(8,128)(2,1)S(1)}, bf16[1232,128]{1,0:T(8,128)(2,1)S(1)}) custom-call(bf16[1232,128]{1,0:T(8,128)(2,1)} %bitcast.7, bf16[1232,128]{1,0:T(8,128)(2,1)} %bitcast.8, bf16[1232,128]{1,0:T(8,128)(2,1)} %bitcast.9, bf16[1232,128]{1,0:T(8,128)(2,1)} %bitcast.10, f32[11,112,112]{2,1,0:T(8,128)} %refs_4_.1, ...), custom_call_target="tpu_custom_call" | custom-call | tf_op jit(solution)/shard_map/scan_kernel/pallas_call | solution.py:501
  44.3 1.0 %place_outputs.1 = (bf16[1232,128]{1,0:T(8,128)(2,1)}, bf16[1232,128]{1,0:T(8,128)(2,1)}, bf16[1232,128]{1,0:T(8,128)(2,1)}) custom-call(bf16[1232,128]{1,0:T(8,128)(2,1)S(1)} %get-tuple-element.9.refs_0_, bf16[1232,128]{1,0:T(8,128)(2,1)S(1)} %get-tuple-element.10.refs_1_, bf16[1232,128]{1,0:T(8,128)(2,1)S(1)} %get-tuple-element.11.refs_2_), custom_call_target="tpu_custom_call" | custom-call | tf_op jit(solution)/shard_map/place_outputs/pallas_call | solution.py:512

commit v6 on v5

--- a/solution.py
+++ b/solution.py
@@ -210,6 +210,16 @@
         at = self.at
         part, sems = self.part(i), self.chunk_s.at[i]
         arrived(self.plane.at[: at.chips - 1, part], sems.at[1])
+        total = self.plane[0, part]
+        for p in range(1, at.chips):
+            total = total + self.plane[p, part]
+        self.column[at.z, part] = total
+        mine = self.column.at[at.z, part]
+        z_send(
+            at,
+            self.later,
+            lambda z: remote(mine, mine, sems.at[2], sems.at[3], at.z_id(z)).start(),
+        )
         order = list(range(at.chips))
         if self.later:
             order.reverse()
@@ -217,13 +227,6 @@
         for p in order:
             self.back[p, part] = running
             running = running + self.plane[p, part]
-        self.column[at.z, part] = running
-        mine = self.column.at[at.z, part]
-        z_send(
-            at,
-            self.later,
-            lambda z: remote(mine, mine, sems.at[2], sems.at[3], at.z_id(z)).start(),
-        )
 
     def back_send(self, i):
         at = self.at

time: 45.6 us -> 45.7 us (level)
  no operation moved by 1% of the time
where the time goes in v6:
time: 45.7 us; the launch traced here: 45.4 us
  Pallas kernels  44.8 us (98%)
  between operations  0.64 us (1%)
    pallas_call x1, Pallas kernels, per_device(): pl.pallas_call(functools.partial(kernel, groups, chips, heads, width, sha...  43.8 us
    pallas_call x1, Pallas kernels, per_device(): pl.pallas_call(place, out_shape=[jax.ShapeDtypeStruct((columns, tokens),...  0.96 us

profile of v6, /device:TPU:1, one launch (start us, length us, event | category | flops | bytes accessed | tf_op | source)
XLA Modules:
  0.0 45.4 jit_solution(16191289736702923144)
XLA Ops:
  0.6 43.8 %scan_kernel.1 = (bf16[1232,128]{1,0:T(8,128)(2,1)S(1)}, bf16[1232,128]{1,0:T(8,128)(2,1)S(1)}, bf16[1232,128]{1,0:T(8,128)(2,1)S(1)}) custom-call(bf16[1232,128]{1,0:T(8,128)(2,1)} %bitcast.7, bf16[1232,128]{1,0:T(8,128)(2,1)} %bitcast.8, bf16[1232,128]{1,0:T(8,128)(2,1)} %bitcast.9, bf16[1232,128]{1,0:T(8,128)(2,1)} %bitcast.10, f32[11,112,112]{2,1,0:T(8,128)} %refs_4_.1, ...), custom_call_target="tpu_custom_call" | custom-call | tf_op jit(solution)/shard_map/scan_kernel/pallas_call | solution.py:504
  44.4 1.0 %place_outputs.1 = (bf16[1232,128]{1,0:T(8,128)(2,1)}, bf16[1232,128]{1,0:T(8,128)(2,1)}, bf16[1232,128]{1,0:T(8,128)(2,1)}) custom-call(bf16[1232,128]{1,0:T(8,128)(2,1)S(1)} %get-tuple-element.9.refs_0_, bf16[1232,128]{1,0:T(8,128)(2,1)S(1)} %get-tuple-element.10.refs_1_, bf16[1232,128]{1,0:T(8,128)(2,1)S(1)} %get-tuple-element.11.refs_2_), custom_call_target="tpu_custom_call" | custom-call | tf_op jit(solution)/shard_map/place_outputs/pallas_call | solution.py:515
